TPU v7x, 128 devices: a whole 4x4x4 slice. The times are simulated.
128 devices in a mesh: dev: 128 (over y, z, x, core).
Axes of the slice: x: 4, y: 4, z: 4, core: 2. Of those that a mesh axis runs over, the one named last changes fastest.
Arguments:
- h_self: bfloat16 [65536, 512], P('dev'), may hold values from -6 to 6
- agg: bfloat16 [65536, 512], P('dev'), may hold values from -6 to 6
- grad_out: bfloat16 [65536, 512], P('dev'), may hold values from -6 to 6
- w_self: bfloat16 [512, 512], replicated, may hold values from -0.25 to 0.25
- w_neigh: bfloat16 [512, 512], replicated, may hold values from -0.25 to 0.25
- owner: int32 [65536, 3, 1], P('dev'), may hold values from 0 to 127; in each aligned block of 1536 rows (0 to 1535, 1536 to 3071, ..., all dimensions but the last counted through in order) at most 18 rows name the same one
- slot: int32 [65536, 3], P('dev'), may hold values from 0 to 2047
- hub_refs: int32 [65536, 2], P('dev'), may hold values from 0 to 1023
Outputs:
- grad_self: bfloat16 [65536, 512], P('dev')
- front_grad: float32 [262144, 512], P('dev')
- hub_grad: float32 [1024, 512], replicated
- grad_w_self: float32 [512, 512], replicated
- grad_w_neigh: float32 [512, 512], replicated
Inputs may be any that keep to these rules, and one draw needn't show every extreme that they name: Among the 1536 references of one device's targets (aligned blocks of rows), no owner is named more than 18 times, a bound that some block reaches.
All inputs are finite; a program needn't handle non-finite values.
Results may differ from a plain program's by a relative error of at most 0.006.
Values may be sent and summed in bfloat16 or wider, within the bound.
No kernel may reach another device: no remote copies, remote signals or barrier semaphores. Data moves between devices by JAX's collectives and lax.ppermute only.
A program may use at most 64 MiB of HBM per device.

v0:
```python
import jax
import jax.numpy as jnp
from jax import lax
from jax.sharding import PartitionSpec as P

OWN_DEV = 2048
HUBS = 1024
FANOUT = 5


def body(h_self, agg, grad_out, w_self, w_neigh, owner, slot, hub_refs):
    rows = h_self.shape[0]
    width = h_self.shape[1]
    count = lax.axis_size("dev")
    fan = slot.shape[1]
    capacity = max(2, (3 * rows * fan + 2 * count - 1) // (2 * count))
    pre = jnp.dot(h_self, w_self, preferred_element_type=jnp.float32) + jnp.dot(
        agg, w_neigh, preferred_element_type=jnp.float32
    )
    sig = jax.nn.sigmoid(pre)
    g = (grad_out.astype(jnp.float32) * (sig * (1.0 + pre * (1.0 - sig)))).astype(jnp.bfloat16)
    scale = 1.0 / jnp.sqrt(jnp.float32(rows * count))
    part_self = jnp.einsum("td,th->dh", h_self, g, preferred_element_type=jnp.float32)
    part_neigh = jnp.einsum("td,th->dh", agg, g, preferred_element_type=jnp.float32)
    grad_self = jnp.einsum("th,dh->td", g, w_self, preferred_element_type=jnp.float32).astype(
        jnp.bfloat16
    )
    message = (
        jnp.einsum("th,dh->td", g, w_neigh, preferred_element_type=jnp.float32) / FANOUT
    ).astype(jnp.bfloat16)
    hub_index = hub_refs.reshape(-1)
    hub_rows = jnp.repeat(message, hub_refs.shape[1], axis=0).astype(jnp.float32)
    hub_part = jnp.zeros((HUBS, width), jnp.float32).at[hub_index].add(hub_rows)
    dest_flat = owner.reshape(-1)
    slot_flat = slot.reshape(-1)
    source_row = jnp.arange(rows * fan, dtype=jnp.int32) // fan
    onehot = (dest_flat[:, None] == jnp.arange(count, dtype=jnp.int32)[None, :]).astype(jnp.int32)
    rank = jnp.sum(jnp.cumsum(onehot, axis=0) * onehot, axis=1) - 1
    sent_slot = jnp.full((count, capacity), OWN_DEV, jnp.int32).at[dest_flat, rank].set(slot_flat)
    sent = (
        jnp.zeros((count, capacity, width), jnp.bfloat16)
        .at[dest_flat, rank]
        .set(message[source_row])
    )
    received, recv_slot = (
        lax.all_to_all(sent, "dev", split_axis=0, concat_axis=0, tiled=True),
        lax.all_to_all(sent_slot, "dev", split_axis=0, concat_axis=0, tiled=True),
    )
    front_grad = (
        jnp.zeros((OWN_DEV, width), jnp.float32)
        .at[recv_slot.reshape(-1)]
        .add(received.reshape(-1, width).astype(jnp.float32), mode="drop")
    )
    hub_grad = lax.psum(hub_part, "dev")
    total_self, total_neigh = lax.psum((part_self, part_neigh), "dev")
    return (grad_self, front_grad, hub_grad, total_self * scale, total_neigh * scale)


def solution(mesh):
    placed = (
        P("dev", None),
        P("dev", None),
        P("dev", None),
        P(),
        P(),
        P("dev", None, None),
        P("dev", None),
        P("dev", None),
    )
    return jax.shard_map(
        body,
        mesh=mesh,
        in_specs=placed,
        out_specs=(P("dev", None), P("dev", None), P(), P(), P()),
        check_vma=False,
    )
```

profile of v0, /device:TPU:1, one launch (start us, length us, event | category | flops | bytes accessed | tf_op | source)
XLA Modules:
  0.0 262.6 jit_solution(15498149804390818128)
XLA Ops:
  7.2 0.9 copy.36
  8.1 0.2 eq.29
  8.5 0.2 reshape.194
  8.8 0.3 fusion.8
  9.3 0.3 copy.40
  9.6 0.5 fusion.10
  10.5 0.2 reshape.234
  10.8 6.2 %scatter_custom_fusion.2 = s32[2304]{0:T(1024)S(1)} fusion(s32[1536]{0:T(1024)S(1)} %broadcast_select_fusion, s32[1536]{0:T(1024)S(1)} %reshape.234, s32[]{:T(128)} %constant.16.clone.1), kind=kCustom, calls=%fused_computation.45 | custom fusion | bytes 9220
  17.0 0.7 copy.42
  17.7 11.5 %all-to-all-start = ((s32[128,1,18]{2,1,0:T(1,128)}), s32[128,1,18]{2,1,0:T(1,128)S(1)}, u32[]{:S(2)}, u32[]{:S(2)}) async-start(s32[128,1,18]{2,1,0:T(1,128)} %copy.42), calls=%async_computation | async-start | bytes 131072 | tf_op jit(solution)/shard_map/all_to_all | solution.py:47
  29.3 0.4 fusion.16
  29.7 0.7 multiply_convert_fusion
  30.5 0.5 fusion.4
  31.0 1.4 convolution_bitcast_fusion
  32.4 1.4 convolution_bitcast_fusion.1
  33.8 0.5 broadcast_in_dim.27
  34.4 2.4 reshape.228
  37.2 8.7 %scatter_custom_fusion.1 = f32[1024,512]{1,0:T(8,128)} fusion(s32[1024]{0:T(1024)S(1)} %bitcast.43, f32[1024,512]{1,0:T(8,128)} %reshape.228, f32[]{:T(128)} %constant.15.clone.1), kind=kCustom, calls=%fused_computation.16 | custom fusion | flops 524288 | bytes 2097664 | tf_op jit(solution)/shard_map/scatter-add | solution.py:33
  45.9 0.2 fusion.13
  46.2 19.2 %scatter_custom_fusion.3 = bf16[2304,512]{1,0:T(8,128)(2,1)S(1)} fusion(s32[1536]{0:T(1024)S(1)} %broadcast_select_fusion, bf16[512,512]{1,0:T(8,128)(2,1)} %copy-done.5, s32[2048]{0:T(1024)S(1)} %pad_clamp_fusion, bf16[]{:T(256)} %constant.11.clone.1), kind=kCustom, calls=%fused_computation.7 | custom fusion | bytes 2359808
  65.3 3.0 %copy.43 = bf16[128,18,512]{2,1,0:T(8,128)(2,1)} copy(bf16[128,18,512]{2,0,1:T(8,128)(2,1)S(1)} %bitcast.40) | data formatting | bytes 4718592 | tf_op jit(solution)/shard_map/scatter | solution.py:43
  68.4 10.4 %all-to-all-start.1 = ((bf16[128,18,512]{2,1,0:T(8,128)(2,1)}), bf16[128,18,512]{2,1,0:T(8,128)(2,1)}, u32[]{:S(2)}, u32[]{:S(2)}) async-start(bf16[128,18,512]{2,1,0:T(8,128)(2,1)} %copy.43), calls=%async_computation.1 | async-start | bytes 6291456 | tf_op jit(solution)/shard_map/all_to_all | solution.py:46
  78.8 1.3 convolution_convert_fusion
  80.0 0.5 broadcast.206
  80.5 0.8 reduce.13
  81.5 144.5 %all-reduce.3.cloned.1.call-done = (f32[1024,512]{1,0:T(8,128)}, f32[512,512]{0,1:T(8,128)}, f32[512,512]{0,1:T(8,128)}) async-done(((f32[1024,512]{1,0:T(8,128)}, f32[512,512]{0,1:T(8,128)}, f32[512,512]{0,1:T(8,128)}), (f32[1024,512]{1,0:T(8,128)}, f32[512,512]{0,1:T(8,128)}, f32[512,512]{0,1:T(8,128)})) %all-reduce.3.cloned.1.call-update) | async-done | bytes 4194320 | tf_op jit(solution)/shard_map/psum | solution.py:54
  226.1 1.8 broadcast_multiply_fusion
  227.9 1.3 copy.45
  229.2 1.3 copy.46
  230.5 5.3 %reshape.220 = f32[2304,512]{1,0:T(8,128)} reshape(bf16[128,18,512]{2,1,0:T(8,128)(2,1)} %all-to-all-done.1) | data formatting | bytes 7077888 | tf_op jit(solution)/shard_map/convert_element_type | solution.py:52
  235.8 18.6 %scatter_custom_fusion = f32[2048,512]{1,0:T(8,128)} fusion(s32[2304]{0:T(1024)S(1)} %fusion.12, f32[2304,512]{1,0:T(8,128)} %reshape.220, f32[]{:T(128)} %constant.15.clone.1), kind=kCustom, calls=%fused_computation.5 | custom fusion | flops 1179648 | bytes 4194816 | tf_op jit(solution)/shard_map/scatter-add | solution.py:52
  254.4 1.3 copy.50
  (45 shorter events, 1.4 us)
Async XLA Ops:
  7.2 22.6 %copy-start = (bf16[512,512]{1,0:T(8,128)(2,1)S(1)}, bf16[512,512]{1,0:T(8,128)(2,1)}, u32[]{:S(2)}) copy-start(bf16[512,512]{1,0:T(8,128)(2,1)} %param.12) | copy-start | bytes 1572868
  9.2 1.0 copy-start.10
  9.2 1.1 copy-start.9
  9.2 1.2 copy-start.7
  9.3 19.9 %copy-start.2 = (bf16[512,512]{1,0:T(8,128)(2,1)S(1)}, bf16[512,512]{1,0:T(8,128)(2,1)}, u32[]{:S(2)}) copy-start(bf16[512,512]{1,0:T(8,128)(2,1)} %param.11) | copy-start | bytes 1572868
  9.3 19.9 %copy-start.4 = (bf16[512,512]{1,0:T(8,128)(2,1)S(1)}, bf16[512,512]{1,0:T(8,128)(2,1)}, u32[]{:S(2)}) copy-start(bf16[512,512]{1,0:T(8,128)(2,1)} %param.8) | copy-start | bytes 1572868
  9.6 20.1 %copy-start.6 = (bf16[512,512]{1,0:T(8,128)(2,1)S(1)}, bf16[512,512]{1,0:T(8,128)(2,1)}, u32[]{:S(2)}) copy-start(bf16[512,512]{1,0:T(8,128)(2,1)} %param.9) | copy-start | bytes 1572868
  9.6 20.1 %copy-start.11 = (bf16[512,512]{1,0:T(8,128)(2,1)S(1)}, bf16[512,512]{1,0:T(8,128)(2,1)}, u32[]{:S(2)}) copy-start(bf16[512,512]{1,0:T(8,128)(2,1)} %param.10) | copy-start | bytes 1572868
  17.7 50.7 %all-to-all-start = ((s32[128,1,18]{2,1,0:T(1,128)}), s32[128,1,18]{2,1,0:T(1,128)S(1)}, u32[]{:S(2)}, u32[]{:S(2)}) async-start(s32[128,1,18]{2,1,0:T(1,128)} %copy.42), calls=%async_computation | async-start | bytes 131072 | tf_op jit(solution)/shard_map/all_to_all | solution.py:47
  29.2 196.9 %all-reduce.3.cloned.1.call-start = ((), (), s32[]{:S(2)}) async-start(), calls=%async_computation.2 | async-start | bytes 8388608 | tf_op jit(solution)/shard_map/psum | solution.py:54
  31.0 2.9 %copy-start.5 = (bf16[512,512]{1,0:T(8,128)(2,1)}, bf16[512,512]{1,0:T(8,128)(2,1)S(1)}, u32[]{:S(2)}) copy-start(bf16[512,512]{1,0:T(8,128)(2,1)S(1)} %fusion.4) | copy-start | bytes 1572868
  34.4 2.5 copy-start.8
  68.4 10.4 %copy-start.3 = (bf16[512,512]{1,0:T(8,128)(2,1)S(1)}, bf16[512,512]{1,0:T(8,128)(2,1)}, u32[]{:S(2)}) copy-start(bf16[512,512]{1,0:T(8,128)(2,1)} %param.11) | copy-start | bytes 1572868
  68.4 162.2 %all-to-all-start.1 = ((bf16[128,18,512]{2,1,0:T(8,128)(2,1)}), bf16[128,18,512]{2,1,0:T(8,128)(2,1)}, u32[]{:S(2)}, u32[]{:S(2)}) async-start(bf16[128,18,512]{2,1,0:T(8,128)(2,1)} %copy.43), calls=%async_computation.1 | async-start | bytes 6291456 | tf_op jit(solution)/shard_map/all_to_all | solution.py:46
  235.8 18.6 %copy-start.1 = (f32[1024,512]{1,0:T(8,128)S(1)}, f32[1024,512]{1,0:T(8,128)}, u32[]{:S(2)}) copy-start(f32[1024,512]{1,0:T(8,128)} %get-tuple-element.36) | copy-start | bytes 6291460
Sparse Core Ops, SparseCore 0:
  46.0 180.0 all-reduce.2
where the time goes:
time: 263 us
  waiting for transfers between devices  145 us (55%)
  local copies, waits for them, and re-layouts  44.6 us (17%)
  other arithmetic  31.3 us (12%)
  starting transfers between devices  21.9 us (8%)
  between operations  14.4 us (5%)
  matrix products  5.76 us (2%)
    psum x1, waiting for transfers between devices, body(): hub_grad = lax.psum(hub_part, 'dev')  145 us
    unnamed x32, local copies, waits for them, and re-layouts  30.5 us
    scatter-add x1, other arithmetic, body(): front_grad = jnp.zeros((OWN_DEV, width), jnp.float32).at[recv_slot.reshap...  18.6 us
    all_to_all x1, starting transfers between devices, body(): lax.all_to_all(sent_slot, 'dev', split_axis=0, concat_axis=0, tiled=True)  11.5 us
    all_to_all x1, starting transfers between devices, body(): lax.all_to_all(sent, 'dev', split_axis=0, concat_axis=0, tiled=True)  10.4 us
    scatter-add x1, other arithmetic, body(): hub_part = jnp.zeros((HUBS, width), jnp.float32).at[hub_index].add(hub_rows)  8.69 us
    convert_element_type x1, local copies, waits for them, and re-layouts, body(): received.reshape(-1, width).astype(jnp.float32)  5.28 us
  transfers between devices with their start and end apart: 3, of which 1 were waited for; matrix products, arithmetic and copies ran while one was open for 18% of the time, Pallas kernels for 0%

commit v1 on v0

v1 whole, which is shorter than its diff:
```python
import functools

import jax
import jax.numpy as jnp
from jax import lax
from jax.experimental import pallas as pl
from jax.experimental.pallas import tpu as pltpu
from jax.sharding import PartitionSpec as P

OWN_DEV = 2048
HUBS = 1024
FANOUT = 5
CAP = 18
MAIN = 16
REST = CAP - MAIN
FRONT = 80
CHUNK = 112
GROUP = 16
VMEM_LIMIT = 50 * 1024 * 1024
BF = jnp.bfloat16
F32 = jnp.float32
I32 = jnp.int32


def mm(a, b):
    return jnp.dot(a, b, preferred_element_type=F32)


def mm_nt(a, b):
    return lax.dot_general(a, b, (((1,), (1,)), ((), ())), preferred_element_type=F32)


def mm_tn(a, b):
    return lax.dot_general(a, b, (((0,), (0,)), ((), ())), preferred_element_type=F32)


def onehot(flag):
    return jnp.where(flag, 1.0, 0.0).astype(BF)


def grads_kernel(me, h, a, go, ws, wn, hub, grad_self, message, mine, send):
    pre = mm(h[...], ws[...]) + mm(a[...], wn[...])
    sig = jax.nn.sigmoid(pre)
    g = (go[...].astype(F32) * (sig * (1.0 + pre * (1.0 - sig)))).astype(BF)
    msg = (mm_nt(g, wn[...]) / FANOUT).astype(BF)
    message[...] = msg
    rows = lax.broadcasted_iota(I32, (HUBS, hub.shape[1]), 0)
    count = onehot(rows == hub[0:1, :]) + onehot(rows == hub[1:2, :])
    hub_part = mm(count, msg).astype(BF)
    depth = h.shape[1]
    first = lax.rem(me[0], 2) == 0
    part_self = mm_tn(h[...], g).astype(BF)
    part_neigh = mm_tn(a[...], g).astype(BF)

    @pl.when(first)
    def _():
        mine[...] = hub_part
        send[0:depth, :] = part_self
        send[depth : 2 * depth, :] = part_neigh

    @pl.when(jnp.logical_not(first))
    def _():
        send[...] = hub_part
        mine[0:depth, :] = part_self
        mine[depth : 2 * depth, :] = part_neigh

    grad_self[...] = mm_nt(g, ws[...]).astype(BF)


def spread_rows(columns):
    row = lax.broadcasted_iota(I32, (GROUP * 16, 192), 0)
    col = lax.broadcasted_iota(I32, (GROUP * 16, 192), 1)
    chunk, s = row // 16, row % 16
    want = jnp.where(s < 8, (s // 2) * 32 + chunk * 2 + s % 2, 128 + (s - 8) * 16 + chunk)
    return onehot((s < 12) & (col == want))


def pack_kernel(me, message, owner, slot, out):
    t = message.shape[0]
    n = out.shape[0]
    fan = owner.shape[0]
    device = lax.broadcasted_iota(I32, (n, t), 0)
    named = [device == owner[j : j + 1, :] for j in range(fan)]
    hot = [onehot(f) for f in named]
    before = onehot(
        lax.broadcasted_iota(I32, (t, t), 0) < lax.broadcasted_iota(I32, (t, t), 1)
    )
    base = jnp.zeros((n, 1), F32)
    ranks = []
    for j in range(fan):
        earlier = mm(hot[j], before) + base
        ranks.append(
            jnp.sum(jnp.where(named[j], earlier, 0.0), axis=0, keepdims=True).astype(I32)
        )
        base = base + jnp.sum(hot[j].astype(F32), axis=1, keepdims=True)
    pos_main = [
        jnp.where(ranks[j] < MAIN, owner[j : j + 1, :] * MAIN + ranks[j], -1) for j in range(fan)
    ]
    pos_rest = [
        jnp.where(ranks[j] >= MAIN, owner[j : j + 1, :] * REST + (ranks[j] - MAIN), -1)
        for j in range(fan)
    ]
    msg = message[...]

    lane = lax.broadcasted_iota(I32, (128, t), 0)
    at_main = (me[0] % 8) * MAIN
    at_rest = (me[0] % 64) * REST - MAIN
    kinds = [jnp.zeros((n, 128), F32) for _ in range(4)]
    for j in range(fan):
        value = slot[j : j + 1, :]
        high, low = (value // 64).astype(F32), (value % 64).astype(F32)
        in_main = ranks[j] < MAIN
        to_main = onehot(in_main & (lane == ranks[j] + at_main))
        to_rest = onehot((ranks[j] >= MAIN) & (lane == ranks[j] + at_rest))
        whole = jnp.where(named[j], 1.0, 0.0)
        a_high, a_low = (whole * high).astype(BF), (whole * low).astype(BF)
        kinds[0] = kinds[0] + mm_nt(a_high, to_main)
        kinds[1] = kinds[1] + mm_nt(a_low, to_main)
        kinds[2] = kinds[2] + mm_nt(a_high, to_rest)
        kinds[3] = kinds[3] + mm_nt(a_low, to_rest)
    kinds = [k.astype(BF) for k in kinds]

    row = lax.broadcasted_iota(I32, (GROUP * MAIN, t), 0)
    rest_row = lax.broadcasted_iota(I32, (n * REST, t), 0)
    rest_pick = (rest_row == pos_rest[0]) | (rest_row == pos_rest[1]) | (rest_row == pos_rest[2])
    rest = mm(onehot(rest_pick), msg).astype(BF)
    spread = spread_rows(192)
    for k in range(n // GROUP):
        at = row + k * GROUP * MAIN
        pick = (at == pos_main[0]) | (at == pos_main[1]) | (at == pos_main[2])
        rows = mm(onehot(pick), msg).astype(BF)
        chunks = pl.ds(k * GROUP, GROUP)
        for q in range(4):
            out[chunks, q * 16 : (q + 1) * 16, :] = rows[:, q * 128 : (q + 1) * 128].reshape(
                GROUP, 16, 128
            )
        stacked = jnp.concatenate(
            [rest[k * 32 : (k + 1) * 32, q * 128 : (q + 1) * 128] for q in range(4)]
            + [kind[k * GROUP : (k + 1) * GROUP, :] for kind in kinds],
            axis=0,
        )
        out[chunks, 64:80, :] = mm(spread, stacked).astype(BF).reshape(GROUP, 16, 128)


def join_kernel(mine, got, held, out):
    q = pl.program_id(0)
    for half in range(2):
        for step in range(2):

            @pl.when(q == step)
            def _():
                at = half * 256 + step * 128
                total = mine[:, at : at + 128].astype(F32) + got[:, at : at + 128].astype(F32)
                out[:, half, :, :] = total.astype(BF).reshape(64, 16, 128)


def reduce_kernel(received, out):
    for half in range(2):
        total = jnp.sum(received[:, half, :, :].astype(F32), axis=0).astype(BF)
        out[:, half, :, :] = jnp.broadcast_to(total[None], (64, 16, 128))


def front_kernel(received, out, rows, index):
    step = pl.program_id(0)
    n = received.shape[0]

    @pl.when(step == 0)
    def _():
        for q in range(4):
            rows[0 : n * MAIN, q * 128 : (q + 1) * 128] = received[
                :, q * 16 : (q + 1) * 16, :
            ].reshape(n * MAIN, 128)
        spread = spread_rows(192)
        main = []
        rest = [jnp.zeros((1, 128), F32), jnp.zeros((1, 128), F32)]
        for k in range(n // GROUP):
            tile = received[k * GROUP : (k + 1) * GROUP, 64:80, :].reshape(GROUP * 16, 128)
            stacked = mm_tn(spread, tile)
            for q in range(4):
                rows[n * MAIN + k * 32 : n * MAIN + (k + 1) * 32, q * 128 : (q + 1) * 128] = (
                    stacked[q * 32 : (q + 1) * 32, :].astype(BF)
                )
            main_slot = stacked[128:144, :] * 64.0 + stacked[144:160, :]
            rest_slot = stacked[160:176, :] * 64.0 + stacked[176:192, :]
            main.append(jnp.sum(main_slot[0:8, :], axis=0, keepdims=True))
            main.append(jnp.sum(main_slot[8:16, :], axis=0, keepdims=True))
            part = k * GROUP // 64
            rest[part] = rest[part] + jnp.sum(rest_slot, axis=0, keepdims=True)
        for g, line in enumerate(main + rest):
            index[g : g + 1, :] = line.astype(I32)

    block = out.shape[0]
    wanted = lax.broadcasted_iota(I32, (block, 128), 0) + step * block
    hot = jnp.concatenate(
        [onehot(wanted == index[g : g + 1, :]) for g in range(n * CAP // 128)], axis=1
    )
    out[...] = mm(hot, rows[...])


def final_kernel(scale, me, own, other, hub_grad, grad_w_self, grad_w_neigh):
    first = lax.rem(me[0], 2) == 0

    def fill(hubs, weights):
        depth = grad_w_self.shape[0]
        for half in range(2):
            for q in range(2):
                at = half * 256 + q * 128
                part = hubs[:, half, q * 16 : (q + 1) * 16, :].reshape(HUBS, 128)
                hub_grad[:, at : at + 128] = part.astype(F32)
                part = weights[:, half, q * 16 : (q + 1) * 16, :].reshape(2 * depth, 128)
                part = part.astype(F32) * scale
                grad_w_self[:, at : at + 128] = part[0:depth, :]
                grad_w_neigh[:, at : at + 128] = part[depth : 2 * depth, :]

    @pl.when(first)
    def _():
        fill(own, other)

    @pl.when(jnp.logical_not(first))
    def _():
        fill(other, own)


SMEM = pl.BlockSpec(memory_space=pltpu.SMEM)
VMEM = pl.BlockSpec(memory_space=pltpu.VMEM)
PARAMS = pltpu.CompilerParams(vmem_limit_bytes=VMEM_LIMIT)


def body(h_self, agg, grad_out, w_self, w_neigh, owner, slot, hub_refs):
    t, width = h_self.shape
    n = lax.axis_size("dev")
    me = lax.axis_index("dev").astype(I32).reshape(1)
    owner_t = owner.reshape(t, -1).T
    slot_t = slot.T
    hub_t = hub_refs.T
    swap = [(i, i ^ 1) for i in range(n)]
    half = jax.ShapeDtypeStruct((HUBS, width), BF)
    same = jax.ShapeDtypeStruct((t, width), BF)

    with jax.named_scope("grads"):
        grad_self, message, mine, send = pl.pallas_call(
            grads_kernel,
            out_shape=(same, same, half, half),
            in_specs=[SMEM] + [VMEM] * 6,
            out_specs=[VMEM] * 4,
            compiler_params=PARAMS,
        )(me, h_self, agg, grad_out, w_self, w_neigh, hub_t)
    with jax.named_scope("core_exchange"):
        got = lax.ppermute(send, "dev", swap)
    with jax.named_scope("pack"):
        packed = pl.pallas_call(
            pack_kernel,
            out_shape=jax.ShapeDtypeStruct((n, CHUNK, 128), BF),
            grid=(1,),
            in_specs=[SMEM] + [VMEM] * 3,
            out_specs=pl.BlockSpec((n, FRONT, 128), lambda i: (0, 0, 0)),
            compiler_params=PARAMS,
        )(me, message, owner_t, slot_t)
    with jax.named_scope("join"):
        packed = pl.pallas_call(
            join_kernel,
            out_shape=jax.ShapeDtypeStruct((n // 2, 2, CHUNK, 128), BF),
            grid=(2,),
            in_specs=[
                pl.BlockSpec((HUBS, width), lambda i: (0, 0)),
                pl.BlockSpec((HUBS, width), lambda i: (0, 0)),
                pl.BlockSpec(memory_space=pl.ANY),
            ],
            out_specs=pl.BlockSpec((n // 2, 2, 16, 128), lambda i: (0, 0, FRONT // 16 + i, 0)),
            input_output_aliases={2: 0},
            compiler_params=PARAMS,
        )(mine, got, packed.reshape(n // 2, 2, CHUNK, 128))
    with jax.named_scope("rows_to_owners"):
        received = lax.all_to_all(
            packed.reshape(n, CHUNK, 128), "dev", split_axis=0, concat_axis=0, tiled=True
        )
    with jax.named_scope("sum_parts"):
        total = pl.pallas_call(
            reduce_kernel,
            out_shape=jax.ShapeDtypeStruct((n // 2, 2, 32, 128), BF),
            grid=(2,),
            in_specs=[
                pl.BlockSpec((n // 2, 2, 16, 128), lambda i: (0, 0, FRONT // 16 + i, 0))
            ],
            out_specs=pl.BlockSpec((n // 2, 2, 16, 128), lambda i: (0, 0, i, 0)),
            compiler_params=PARAMS,
        )(received.reshape(n // 2, 2, CHUNK, 128))
    with jax.named_scope("sums_to_all"):
        own = lax.all_to_all(
            total.reshape(n, 32, 128), "dev", split_axis=0, concat_axis=0, tiled=True
        )
    with jax.named_scope("front"):
        front_grad = pl.pallas_call(
            front_kernel,
            out_shape=jax.ShapeDtypeStruct((OWN_DEV, width), F32),
            grid=(8,),
            in_specs=[pl.BlockSpec((n, FRONT, 128), lambda i: (0, 0, 0))],
            out_specs=pl.BlockSpec((OWN_DEV // 8, width), lambda i: (i, 0)),
            scratch_shapes=[
                pltpu.VMEM((n * CAP, width), BF),
                pltpu.VMEM((24, 128), I32),
            ],
            compiler_params=PARAMS,
            cost_estimate=pl.CostEstimate(
                flops=2 * OWN_DEV * n * CAP * width, bytes_accessed=8 << 20, transcendentals=0
            ),
        )(received)
    with jax.named_scope("core_exchange_back"):
        other = lax.ppermute(own, "dev", swap)
    scale = 1.0 / (t * n) ** 0.5
    with jax.named_scope("final"):
        hub_grad, grad_w_self, grad_w_neigh = pl.pallas_call(
            functools.partial(final_kernel, scale),
            out_shape=(
                jax.ShapeDtypeStruct((HUBS, width), F32),
                jax.ShapeDtypeStruct((width, width), F32),
                jax.ShapeDtypeStruct((width, width), F32),
            ),
            in_specs=[SMEM, VMEM, VMEM],
            out_specs=[VMEM] * 3,
            compiler_params=PARAMS,
        )(me, own.reshape(n // 2, 2, 32, 128), other.reshape(n // 2, 2, 32, 128))
    return grad_self, front_grad, hub_grad, grad_w_self, grad_w_neigh


def solution(mesh):
    placed = (
        P("dev", None),
        P("dev", None),
        P("dev", None),
        P(),
        P(),
        P("dev", None, None),
        P("dev", None),
        P("dev", None),
    )
    return jax.shard_map(
        body,
        mesh=mesh,
        in_specs=placed,
        out_specs=(P("dev", None), P("dev", None), P(), P(), P()),
        check_vma=False,
    )
```

time: 263 us -> 114 us (0.43)
  waiting for transfers between devices: 145 us -> 0.01 us
  blocking collectives: 0 us -> 81.5 us
  local copies, waits for them, and re-layouts: 44.6 us -> 7.28 us
  other arithmetic: 31.3 us -> 0 us
  Pallas kernels: 0 us -> 22 us
  starting transfers between devices: 21.9 us -> 2.28 us
  between operations: 14.4 us -> 0.67 us
  matrix products: 5.76 us -> 0 us
    psum x1 -> x0, waiting for transfers between devices: 145 us -> none  [body(): hub_grad = lax.psum(hub_part, 'dev')]
    all_to_all x0 -> x2, blocking collectives: none -> 81.5 us  [the longest x1 57.8 us: body(): lax.all_to_all(packed.reshape(n, CHUNK, 128), 'dev', split_axis=0, concat...]
    scatter-add x2 -> x0, other arithmetic: 27.3 us -> none  [the longest x1 18.6 us: body(): front_grad = jnp.zeros((OWN_DEV, width), jnp.float32).at[recv_slot.reshap...]
    unnamed x32 -> x19, local copies, waits for them, and re-layouts: 30.5 us -> 7.28 us
    pallas_call x0 -> x6, Pallas kernels: none -> 22 us  [the longest x1 8.01 us: body(): pl.pallas_call(front_kernel, out_shape=jax.ShapeDtypeStruct((OWN_DEV, wid...]
    all_to_all x2 -> x0, starting transfers between devices: 21.9 us -> none  [the longest x1 11.5 us: body(): lax.all_to_all(sent_slot, 'dev', split_axis=0, concat_axis=0, tiled=True)]
    convert_element_type x2 -> x0, local copies, waits for them, and re-layouts: 7.72 us -> none  [the longest x1 5.28 us: body(): received.reshape(-1, width).astype(jnp.float32)]
    dot_general x6 -> x0, matrix products: 5.76 us -> none  [the longest x1 1.43 us: body(): jnp.einsum('td,th->dh', agg, g, preferred_element_type=jnp.float32)]
  transfers between devices with their start and end apart: 3 -> 2, of which waited for: 1 -> 0; matrix products, arithmetic and copies ran while one was open for 18% -> 1% of each run, Pallas kernels for 0% -> 11%
where the time goes in v1:
time: 114 us
  blocking collectives  81.5 us (71%)
  Pallas kernels  22 us (19%)
  local copies, waits for them, and re-layouts  7.28 us (6%)
  starting transfers between devices  2.28 us (2%)
    all_to_all x1, blocking collectives, body(): lax.all_to_all(packed.reshape(n, CHUNK, 128), 'dev', split_axis=0, concat...  57.8 us
    all_to_all x1, blocking collectives, body(): lax.all_to_all(total.reshape(n, 32, 128), 'dev', split_axis=0, concat_axi...  23.7 us
    pallas_call x1, Pallas kernels, body(): pl.pallas_call(front_kernel, out_shape=jax.ShapeDtypeStruct((OWN_DEV, wid...  8.01 us
    unnamed x19, local copies, waits for them, and re-layouts  7.28 us
    pallas_call x1, Pallas kernels, body(): pl.pallas_call(pack_kernel, out_shape=jax.ShapeDtypeStruct((n, CHUNK, 128...  4.49 us
    pallas_call x1, Pallas kernels, body(): pl.pallas_call(grads_kernel, out_shape=(same, same, half, half), in_specs...  4.11 us
    pallas_call x1, Pallas kernels, body(): pl.pallas_call(functools.partial(final_kernel, scale), out_shape=(jax.Sha...  2.65 us
  transfers between devices with their start and end apart: 2, of which 0 were waited for; matrix products, arithmetic and copies ran while one was open for 1% of the time, Pallas kernels for 11%

profile of v1, /device:TPU:1, one launch (start us, length us, event | category | flops | bytes accessed | tf_op | source)
XLA Modules:
  0.0 113.7 jit_solution(431262201571085210)
XLA Ops:
  0.6 0.0 copy-start.2
  0.6 1.0 copy-done.2
  1.7 0.0 copy-start.3
  1.7 1.0 copy-done.3
  2.7 0.0 copy-start.4
  2.7 1.0 copy-done.4
  3.8 0.0 copy-start.5
  3.8 1.0 copy-done.5
  4.8 0.0 copy-start.6
  4.8 1.0 copy-done.6
  5.8 0.0 copy-start.8
  5.8 0.7 copy-done.8
  6.5 4.1 %grads.1 = (bf16[512,512]{1,0:T(8,128)(2,1)}, bf16[512,512]{1,0:T(8,128)(2,1)S(1)}, bf16[1024,512]{1,0:T(8,128)(2,1)}, bf16[1024,512]{1,0:T(8,128)(2,1)}) custom-call(s32[1]{0:T(128)} %bitcast.me, bf16[512,512]{1,0:T(8,128)(2,1)S(1)} %copy-done.2, bf16[512,512]{1,0:T(8,128)(2,1)S(1)} %copy-done.3, bf16[512,512]{1,0:T(8,128)(2,1)S(1)} %copy-done.4, ...), custom_call_target="tpu_custom_call" | custom-call | tf_op jit(solution)/shard_map/grads/pallas_call | solution.py:241
  10.6 0.0 copy-start.1
  10.6 1.4 %collective-permute-start = (bf16[1024,512]{1,0:T(8,128)(2,1)}, bf16[1024,512]{1,0:T(8,128)(2,1)S(1)}, u32[]{:S(2)}, u32[]{:S(2)}) collective-permute-start(bf16[1024,512]{1,0:T(8,128)(2,1)} %get-tuple-element.14), channel_id=1, source_target_pairs={{0,1},{1,0},{2,3},{3,2},{4,5},{5,4},{6,7},{7,6},{8,9},{9,8},{10,11... | collective-permute-start | bytes 3145736 | tf_op jit(solution)/shard_map/core_exchange/ppermute | solution.py:249
  12.1 0.7 copy.16
  12.8 0.0 copy-start.7
  12.8 0.7 copy-done.7
  13.5 4.5 %pack.1 = bf16[128,112,128]{2,1,0:T(8,128)(2,1)} custom-call(s32[1]{0:T(128)} %bitcast.me, bf16[512,512]{1,0:T(8,128)(2,1)S(1)} %get-tuple-element.15.message, s32[3,512]{1,0:T(4,128)S(1)} %bitcast.18, s32[3,512]{1,0:T(4,128)S(1)} %bitcast.19), custom_call_target="tpu_custom_call" | custom-call | tf_op jit(solution)/shard_map/pack/pallas_call | solution.py:251
  17.9 0.0 collective-permute-done.got
  17.9 0.0 copy-done.1
  18.0 1.1 join.1
  19.1 57.8 %all_to_all.10.received = bf16[128,112,128]{2,1,0:T(8,128)(2,1)} all-to-all(bf16[128,112,128]{2,1,0:T(8,128)(2,1)} %bitcast.22), channel_id=1, replica_groups=mesh['dev'=128] {'dev'}, dimensions={0} | all-to-all | bytes 7340032 | tf_op jit(solution)/shard_map/rows_to_owners/all_to_all | solution.py:274
  76.8 0.0 copy-start
  76.8 1.6 %sum_parts.1 = bf16[64,2,32,128]{3,2,1,0:T(8,128)(2,1)S(1)} custom-call(bf16[64,2,112,128]{3,2,1,0:T(8,128)(2,1)} %bitcast.14), custom_call_target="tpu_custom_call" | custom-call | tf_op jit(solution)/shard_map/sum_parts/pallas_call | solution.py:278
  78.4 23.7 %all_to_all.11 = bf16[128,32,128]{2,1,0:T(8,128)(2,1)S(1)} all-to-all(bf16[128,32,128]{2,1,0:T(8,128)(2,1)S(1)} %bitcast.16), channel_id=1, replica_groups=mesh['dev'=128] {'dev'}, dimensions={0} | all-to-all | bytes 2097152 | tf_op jit(solution)/shard_map/sums_to_all/all_to_all | solution.py:289
  102.2 0.9 collective-permute-start.1
  103.0 0.0 copy-done
  103.0 8.0 %front.1 = f32[2048,512]{1,0:T(8,128)} custom-call(bf16[128,112,128]{2,1,0:T(8,128)(2,1)S(1)} %copy-done), custom_call_target="tpu_custom_call" | custom-call | flops 4831838208 | bytes 8388608 | tf_op jit(solution)/shard_map/front/pallas_call | solution.py:293
  111.0 0.0 collective-permute-done.1
  111.1 2.7 %final.1 = (f32[1024,512]{1,0:T(8,128)}, f32[512,512]{1,0:T(8,128)}, f32[512,512]{1,0:T(8,128)}) custom-call(s32[1]{0:T(128)} %bitcast.me, bf16[64,2,32,128]{3,2,1,0:T(8,128)(2,1)S(1)} %bitcast.15, bf16[64,2,32,128]{3,2,1,0:T(8,128)(2,1)S(1)} %bitcast.17), custom_call_target="tpu_custom_call" | custom-call | tf_op jit(solution)/shard_map/final/pallas_call | solution.py:312
Async XLA Ops:
  0.6 1.0 copy-start.2
  1.7 1.0 copy-start.3
  2.7 1.0 copy-start.4
  3.8 1.0 copy-start.5
  4.8 1.0 copy-start.6
  5.8 0.7 copy-start.8
  10.6 7.3 %copy-start.1 = (bf16[1024,512]{1,0:T(8,128)(2,1)S(1)}, bf16[1024,512]{1,0:T(8,128)(2,1)}, u32[]{:S(2)}) copy-start(bf16[1024,512]{1,0:T(8,128)(2,1)} %get-tuple-element.13.mine) | copy-start | bytes 3145732
  10.6 7.3 %collective-permute-start = (bf16[1024,512]{1,0:T(8,128)(2,1)}, bf16[1024,512]{1,0:T(8,128)(2,1)S(1)}, u32[]{:S(2)}, u32[]{:S(2)}) collective-permute-start(bf16[1024,512]{1,0:T(8,128)(2,1)} %get-tuple-element.14), channel_id=1, source_target_pairs={{0,1},{1,0},{2,3},{3,2},{4,5},{5,4},{6,7},{7,6},{8,9},{9,8},{10,11... | collective-permute-start | bytes 3145736 | tf_op jit(solution)/shard_map/core_exchange/ppermute | solution.py:249
  12.8 0.7 copy-start.7
  76.8 26.2 %copy-start = (bf16[128,112,128]{2,1,0:T(8,128)(2,1)S(1)}, bf16[128,112,128]{2,1,0:T(8,128)(2,1)}, u32[]{:S(2)}) copy-start(bf16[128,112,128]{2,1,0:T(8,128)(2,1)} %all_to_all.10.received) | copy-start | bytes 11010052
  102.2 8.9 %collective-permute-start.1 = (bf16[128,32,128]{2,1,0:T(8,128)(2,1)S(1)}, bf16[128,32,128]{2,1,0:T(8,128)(2,1)S(1)}, u32[]{:S(2)}, u32[]{:S(2)}) collective-permute-start(bf16[128,32,128]{2,1,0:T(8,128)(2,1)S(1)} %all_to_all.11), channel_id=1, source_target_pairs={{0,1},{1,0},{2,3},{3,2},{4,5},{5,4},{6,7},{7,6},{8,9},{9,8},{10,11... | collective-permute-start | bytes 3145736 | tf_op jit(solution)/shard_map/core_exchange_back/ppermute | solution.py:309

commit v2 on v1

v2 whole, which is shorter than its diff:
```python
import functools

import jax
import jax.numpy as jnp
from jax import lax
from jax.experimental import pallas as pl
from jax.experimental.pallas import tpu as pltpu
from jax.sharding import PartitionSpec as P

OWN_DEV = 2048
HUBS = 1024
FANOUT = 5
CAP = 18
MAIN = 16
REST = CAP - MAIN
FRONT = 80
CHUNK = 112
GROUP = 16
VMEM_LIMIT = 28 * 1024 * 1024
BF = jnp.bfloat16
F32 = jnp.float32
I32 = jnp.int32


def mm(a, b):
    return jnp.dot(a, b, preferred_element_type=F32)


def mm_nt(a, b):
    return lax.dot_general(a, b, (((1,), (1,)), ((), ())), preferred_element_type=F32)


def mm_tn(a, b):
    return lax.dot_general(a, b, (((0,), (0,)), ((), ())), preferred_element_type=F32)


def onehot(flag):
    return jnp.where(flag, 1.0, 0.0).astype(BF)


def slot_kinds(me, slot, named, ranks):
    t = named[0].shape[1]
    lane = lax.broadcasted_iota(I32, (256, t), 0)
    at_main = (me % 8) * MAIN
    at_rest = (me % 64) * REST - MAIN + 128
    values, lanes = [], []
    for j, rank in enumerate(ranks):
        value = slot[j]
        high, low = (value // 64).astype(F32), (value % 64).astype(F32)
        values.append(
            jnp.concatenate(
                [jnp.where(named[j], high, 0.0), jnp.where(named[j], low, 0.0)], axis=0
            ).astype(BF)
        )
        lanes.append(onehot(lane == rank + jnp.where(rank < MAIN, at_main, at_rest)))
    return mm_nt(jnp.concatenate(values, axis=1), jnp.concatenate(lanes, axis=1))


def grads_kernel(
    me, h_in, a_in, go_in, ws_in, wn_in, owner_in, slot_in, hub_in,
    grad_self, message, mine, send, places, kinds,
    h, a, go, ws, wn, owner, slot, hub, back, arrived,
):
    loads = [
        pltpu.make_async_copy(src, dst, arrived.at[i])
        for i, (src, dst) in enumerate(
            (
                (owner_in, owner), (slot_in, slot), (hub_in, hub),
                (h_in, h), (ws_in, ws), (a_in, a), (wn_in, wn), (go_in, go),
            )
        )
    ]
    for load in loads:
        load.start()

    t = h.shape[0]
    n = kinds.shape[1]
    fan = slot.shape[0]
    device = lax.broadcasted_iota(I32, (n, t), 0)
    before = onehot(lax.broadcasted_iota(I32, (t, t), 0) < lax.broadcasted_iota(I32, (t, t), 1))
    loads[0].wait()
    loads[1].wait()
    named = [device == owner[j] for j in range(fan)]
    slots = [slot[j : j + 1, :] for j in range(fan)]
    hot = jnp.concatenate([onehot(f) for f in named], axis=0)
    earlier = mm(hot, before)
    amount = jnp.sum(hot.astype(F32), axis=1, keepdims=True)
    base = jnp.zeros((n, 1), F32)
    ranks = []
    for j in range(fan):
        rank = jnp.where(named[j], earlier[j * n : (j + 1) * n, :] + base, 0.0)
        ranks.append(jnp.sum(rank, axis=0, keepdims=True).astype(I32))
        base = base + amount[j * n : (j + 1) * n, :]
    for j in range(fan):
        in_main = ranks[j] < MAIN
        places[j : j + 1, :] = jnp.where(in_main, owner[j] * MAIN + ranks[j], -1)
        places[4 + j : 5 + j, :] = jnp.where(in_main, -1, owner[j] * REST + (ranks[j] - MAIN))
    kind = slot_kinds(me[0], slots, named, ranks).astype(BF)
    for i in range(4):
        kinds[i] = kind[(i % 2) * n : (i % 2 + 1) * n, (i // 2) * 128 : (i // 2 + 1) * 128]
    loads[2].wait()
    rows = lax.broadcasted_iota(I32, (HUBS, t), 0)
    count = onehot(rows == hub[0:1, :]) + onehot(rows == hub[1:2, :])

    loads[3].wait()
    loads[4].wait()
    pre = mm(h[...], ws[...])
    loads[5].wait()
    loads[6].wait()
    pre = pre + mm(a[...], wn[...])
    loads[7].wait()
    sig = jax.nn.sigmoid(pre)
    g = (go[...].astype(F32) * (sig * (1.0 + pre * (1.0 - sig)))).astype(BF)
    back[...] = mm_nt(g, ws[...]).astype(BF)
    store = pltpu.make_async_copy(back, grad_self, arrived.at[8])
    store.start()
    msg = (mm_nt(g, wn[...]) / FANOUT).astype(BF)
    message[...] = msg
    hub_part = mm(count, msg).astype(BF)
    depth = h.shape[1]
    first = lax.rem(me[0], 2) == 0
    part_self = mm_tn(h[...], g).astype(BF)
    part_neigh = mm_tn(a[...], g).astype(BF)

    @pl.when(first)
    def _():
        mine[...] = hub_part
        send[0:depth, :] = part_self
        send[depth : 2 * depth, :] = part_neigh

    @pl.when(jnp.logical_not(first))
    def _():
        send[...] = hub_part
        mine[0:depth, :] = part_self
        mine[depth : 2 * depth, :] = part_neigh

    store.wait()


def spread_rows():
    row = lax.broadcasted_iota(I32, (GROUP * 16, 192), 0)
    col = lax.broadcasted_iota(I32, (GROUP * 16, 192), 1)
    chunk, s = row // 16, row % 16
    want = jnp.where(s < 8, (s // 2) * 32 + chunk * 2 + s % 2, 128 + (s - 8) * 16 + chunk)
    return onehot((s < 12) & (col == want))


def picks(places, first, at):
    flag = at == places[first : first + 1, :]
    for j in range(first + 1, first + 3):
        flag = flag | (at == places[j : j + 1, :])
    return onehot(flag)


def pack_kernel(places, kinds, message, out):
    t = message.shape[0]
    chunks = out.shape[0]
    spread = spread_rows()
    msg = message[...]
    at = lax.broadcasted_iota(I32, (chunks * MAIN, t), 0)
    rows = mm(picks(places, 0, at), msg).astype(BF)
    for q in range(4):
        out[:, q * 16 : (q + 1) * 16, :] = rows[:, q * 128 : (q + 1) * 128].reshape(
            chunks, 16, 128
        )
    at = lax.broadcasted_iota(I32, (chunks * REST, t), 0)
    rest = mm(picks(places, 4, at), msg).astype(BF)
    for g in range(chunks // GROUP):
        stacked = jnp.concatenate(
            [rest[g * 32 : (g + 1) * 32, q * 128 : (q + 1) * 128] for q in range(4)]
            + [kinds[i, g * GROUP : (g + 1) * GROUP, :] for i in range(4)],
            axis=0,
        )
        out[g * GROUP : (g + 1) * GROUP, 64:80, :] = (
            mm(spread, stacked).astype(BF).reshape(GROUP, 16, 128)
        )


def join_kernel(mine, got, held, out):
    for half in range(2):
        for q in range(2):
            at = half * 256 + q * 128
            total = mine[:, at : at + 128].astype(F32) + got[:, at : at + 128].astype(F32)
            first = FRONT + q * 16
            out[:, half, first : first + 16, :] = total.astype(BF).reshape(-1, 16, 128)


def reduce_kernel(received, out, parts, total, arrived, left):
    chips = parts.shape[0]
    steps, copies = arrived.shape[0], left.shape[0]
    piece, each = chips // steps, total.shape[0]
    loads = [
        pltpu.make_async_copy(
            received.at[pl.ds(i * piece, piece), :, pl.ds(FRONT, 32), :],
            parts.at[pl.ds(i * piece, piece)],
            arrived.at[i],
        )
        for i in range(steps)
    ]
    for load in loads:
        load.start()
    acc = jnp.zeros((1, 2, 32, 128), F32)
    for i, load in enumerate(loads):
        load.wait()
        block = parts[i * piece : (i + 1) * piece].astype(F32)
        acc = acc + jnp.sum(block, axis=0, keepdims=True)
    total[...] = jnp.broadcast_to(acc.astype(BF), total.shape)
    stores = [
        pltpu.make_async_copy(total, out.at[pl.ds(i * each, each)], left.at[i])
        for i in range(copies)
    ]
    for store in stores:
        store.start()
    for store in stores:
        store.wait()


def front_kernel(received, out, rows, index):
    step = pl.program_id(0)
    n = received.shape[0]

    @pl.when(step == 0)
    def _():
        for q in range(4):
            rows[0 : n * MAIN, q * 128 : (q + 1) * 128] = received[
                :, q * 16 : (q + 1) * 16, :
            ].reshape(n * MAIN, 128)
        spread = spread_rows()
        main = []
        rest = [jnp.zeros((1, 128), F32), jnp.zeros((1, 128), F32)]
        for k in range(n // GROUP):
            tile = received[k * GROUP : (k + 1) * GROUP, 64:80, :].reshape(GROUP * 16, 128)
            stacked = mm_tn(spread, tile)
            for q in range(4):
                rows[n * MAIN + k * 32 : n * MAIN + (k + 1) * 32, q * 128 : (q + 1) * 128] = (
                    stacked[q * 32 : (q + 1) * 32, :].astype(BF)
                )
            main_slot = stacked[128:144, :] * 64.0 + stacked[144:160, :]
            rest_slot = stacked[160:176, :] * 64.0 + stacked[176:192, :]
            main.append(jnp.sum(main_slot[0:8, :], axis=0, keepdims=True))
            main.append(jnp.sum(main_slot[8:16, :], axis=0, keepdims=True))
            part = k * GROUP // 64
            rest[part] = rest[part] + jnp.sum(rest_slot, axis=0, keepdims=True)
        for g, line in enumerate(main + rest):
            index[g : g + 1, :] = line.astype(I32)

    block = out.shape[0]
    wanted = lax.broadcasted_iota(I32, (block, 128), 0) + step * block
    hot = jnp.concatenate(
        [onehot(wanted == index[g : g + 1, :]) for g in range(n * CAP // 128)], axis=1
    )
    out[...] = mm(hot, rows[...])


def fill_kernel(scale, mine, me, part, *refs):
    hub_grad, grad_w_self, grad_w_neigh, wide, done = refs[-5:]
    depth = grad_w_self.shape[0]
    hubs = (lax.rem(me[0], 2) == 0) == mine
    factor = jnp.where(hubs, 1.0, scale)
    steps = 4
    rows = HUBS // steps
    chips = rows // 16

    def copies(step):
        src = wide.at[pl.ds(step * rows, rows)]
        to_hubs = hub_grad.at[pl.ds(step * rows, rows)]
        weights = grad_w_self if step < steps // 2 else grad_w_neigh
        to_weights = weights.at[pl.ds(step * rows % depth, rows)]
        return (
            pltpu.make_async_copy(src, to_hubs, done.at[step]),
            pltpu.make_async_copy(src, to_weights, done.at[step]),
        )

    for step in range(steps):
        for half in range(2):
            for q in range(2):
                at = half * 256 + q * 128
                block = part[step * chips : (step + 1) * chips, half, q * 16 : (q + 1) * 16, :]
                wide[step * rows : (step + 1) * rows, at : at + 128] = (
                    block.reshape(rows, 128).astype(F32) * factor
                )
        to_hubs, to_weights = copies(step)
        pl.when(hubs)(to_hubs.start)
        pl.when(jnp.logical_not(hubs))(to_weights.start)
    for step in range(steps):
        to_hubs, to_weights = copies(step)
        pl.when(hubs)(to_hubs.wait)
        pl.when(jnp.logical_not(hubs))(to_weights.wait)


SMEM = pl.BlockSpec(memory_space=pltpu.SMEM)
HBM = pl.BlockSpec(memory_space=pltpu.HBM)
VMEM = pl.BlockSpec(memory_space=pltpu.VMEM)
PARAMS = pltpu.CompilerParams(vmem_limit_bytes=VMEM_LIMIT)


def in_hbm(x):
    return pltpu.with_memory_space_constraint(x, pltpu.HBM)


def in_vmem(x):
    return pltpu.with_memory_space_constraint(x, pltpu.VMEM)


def body(h_self, agg, grad_out, w_self, w_neigh, owner, slot, hub_refs):
    t, width = h_self.shape
    n = lax.axis_size("dev")
    me = lax.axis_index("dev").astype(I32).reshape(1)
    owner_t = owner.transpose(1, 2, 0)
    slot_t = slot.T
    hub_t = hub_refs.T
    swap = [(i, i ^ 1) for i in range(n)]
    half = jax.ShapeDtypeStruct((HUBS, width), BF)
    same = jax.ShapeDtypeStruct((t, width), BF)

    fan = slot.shape[1]
    with jax.named_scope("grads"):
        grad_self, message, mine, send, places, kinds = pl.pallas_call(
            grads_kernel,
            out_shape=(
                pltpu.HBM((t, width), BF),
                pltpu.VMEM((t, width), BF),
                pltpu.VMEM((HUBS, width), BF),
                pltpu.VMEM((HUBS, width), BF),
                pltpu.VMEM((8, t), I32),
                pltpu.VMEM((4, n, 128), BF),
            ),
            in_specs=[SMEM] + [HBM] * 8,
            out_specs=[HBM] + [VMEM] * 5,
            scratch_shapes=[pltpu.VMEM((t, width), BF)] * 3
            + [pltpu.VMEM((width, width), BF)] * 2
            + [
                pltpu.VMEM((fan, 1, t), I32),
                pltpu.VMEM((fan, t), I32),
                pltpu.VMEM(hub_t.shape, I32),
                pltpu.VMEM((t, width), BF),
                pltpu.SemaphoreType.DMA((9,)),
            ],
            compiler_params=PARAMS,
        )(me, *map(in_hbm, (h_self, agg, grad_out, w_self, w_neigh, owner_t, slot_t, hub_t)))
    with jax.named_scope("core_exchange"):
        got = lax.ppermute(send, "dev", swap)
    with jax.named_scope("pack"):
        packed = pl.pallas_call(
            pack_kernel,
            out_shape=pltpu.VMEM((n, CHUNK, 128), BF),
            in_specs=[VMEM] * 3,
            out_specs=VMEM,
            compiler_params=PARAMS,
        )(*map(in_vmem, (places, kinds, message)))
    with jax.named_scope("join"):
        packed = pl.pallas_call(
            join_kernel,
            out_shape=pltpu.VMEM((n // 2, 2, CHUNK, 128), BF),
            in_specs=[VMEM, VMEM, HBM],
            out_specs=VMEM,
            input_output_aliases={2: 0},
            compiler_params=PARAMS,
        )(in_vmem(mine), in_vmem(got), in_vmem(packed.reshape(n // 2, 2, CHUNK, 128)))
    with jax.named_scope("rows_to_owners"):
        received = lax.all_to_all(
            packed.reshape(n, CHUNK, 128), "dev", split_axis=0, concat_axis=0, tiled=True
        )
    with jax.named_scope("sum_parts"):
        total = pl.pallas_call(
            reduce_kernel,
            out_shape=pltpu.HBM((n // 2, 2, 32, 128), BF),
            in_specs=[HBM],
            out_specs=HBM,
            scratch_shapes=[
                pltpu.VMEM((n // 2, 2, 32, 128), BF),
                pltpu.VMEM((8, 2, 32, 128), BF),
                pltpu.SemaphoreType.DMA((4,)),
                pltpu.SemaphoreType.DMA((n // 16,)),
            ],
            compiler_params=PARAMS,
        )(in_hbm(received.reshape(n // 2, 2, CHUNK, 128)))
    with jax.named_scope("sums_to_all"):
        own = lax.all_to_all(
            total.reshape(n, 32, 128), "dev", split_axis=0, concat_axis=0, tiled=True
        )
    with jax.named_scope("front"):
        front_grad = pl.pallas_call(
            front_kernel,
            out_shape=jax.ShapeDtypeStruct((OWN_DEV, width), F32),
            grid=(8,),
            in_specs=[pl.BlockSpec((n, FRONT, 128), lambda i: (0, 0, 0))],
            out_specs=pl.BlockSpec((OWN_DEV // 8, width), lambda i: (i, 0)),
            scratch_shapes=[
                pltpu.VMEM((n * CAP, width), BF),
                pltpu.VMEM((24, 128), I32),
            ],
            compiler_params=PARAMS,
            cost_estimate=pl.CostEstimate(
                flops=2 * OWN_DEV * n * CAP * width, bytes_accessed=8 << 20, transcendentals=0
            ),
        )(in_hbm(received))
    own, front_grad = lax.optimization_barrier((own, front_grad))
    with jax.named_scope("core_exchange_back"):
        other = lax.ppermute(own, "dev", swap)
    scale = 1.0 / (t * n) ** 0.5
    filled = ()
    for mine_too, part in ((True, own), (False, other)):
        with jax.named_scope("fill_own" if mine_too else "fill_other"):
            filled = pl.pallas_call(
                functools.partial(fill_kernel, scale, mine_too),
                out_shape=(
                    jax.ShapeDtypeStruct((HUBS, width), F32),
                    jax.ShapeDtypeStruct((width, width), F32),
                    jax.ShapeDtypeStruct((width, width), F32),
                ),
                in_specs=[SMEM, VMEM] + [HBM] * len(filled),
                out_specs=[HBM] * 3,
                scratch_shapes=[pltpu.VMEM((HUBS, width), F32), pltpu.SemaphoreType.DMA((4,))],
                input_output_aliases={2 + i: i for i in range(len(filled))},
                compiler_params=PARAMS,
                cost_estimate=pl.CostEstimate(
                    flops=HUBS * width, bytes_accessed=3 << 20, transcendentals=0
                ),
            )(me, part.reshape(n // 2, 2, 32, 128), *filled)
    hub_grad, grad_w_self, grad_w_neigh = filled
    return grad_self, front_grad, hub_grad, grad_w_self, grad_w_neigh


def solution(mesh):
    placed = (
        P("dev", None),
        P("dev", None),
        P("dev", None),
        P(),
        P(),
        P("dev", None, None),
        P("dev", None),
        P("dev", None),
    )
    return jax.shard_map(
        body,
        mesh=mesh,
        in_specs=placed,
        out_specs=(P("dev", None), P("dev", None), P(), P(), P()),
        check_vma=False,
    )
```

time: 114 us -> 99.9 us (0.88)
  blocking collectives: 81.5 us -> 57.8 us
  waiting for transfers between devices: 0.01 us -> 10.7 us
  local copies, waits for them, and re-layouts: 7.28 us -> 0 us
  starting transfers between devices: 2.28 us -> 6.97 us
  Pallas kernels: 22 us -> 23.5 us
    all_to_all x1 -> x0, blocking collectives: 23.7 us -> none  [body(): lax.all_to_all(total.reshape(n, 32, 128), 'dev', split_axis=0, concat_axi...]
    all_to_all x0 -> x1, waiting for transfers between devices: none -> 9.65 us  [body(): lax.all_to_all(total.reshape(n, 32, 128), 'dev', split_axis=0, concat_axi...]
    unnamed x19 -> x0, local copies, waits for them, and re-layouts: 7.28 us -> none
    all_to_all x0 -> x1, starting transfers between devices: none -> 4.6 us  [body(): lax.all_to_all(total.reshape(n, 32, 128), 'dev', split_axis=0, concat_axi...]
    pallas_call x1, Pallas kernels: 8.01 us -> 9.69 us  [body(): pl.pallas_call(front_kernel, out_shape=jax.ShapeDtypeStruct((OWN_DEV, wid...]
    pallas_call x5 -> x6, Pallas kernels: 14 us -> 13.8 us  [the longest x1 6.37 us: body(): pl.pallas_call(grads_kernel, out_shape=(pltpu.HBM((t, width), BF), pltpu....]
  transfers between devices with their start and end apart: 2 -> 3, of which waited for: 0 -> 3; matrix products, arithmetic and copies ran while one was open for 1% -> 0% of each run, Pallas kernels for 11% -> 13%
where the time goes in v2:
time: 99.9 us; the launch traced here: 99.7 us
  blocking collectives  57.8 us (58%)
  Pallas kernels  23.5 us (24%)
  waiting for transfers between devices  10.7 us (11%)
  starting transfers between devices  6.97 us (7%)
    all_to_all x1, blocking collectives, body(): lax.all_to_all(packed.reshape(n, CHUNK, 128), 'dev', split_axis=0, concat...  57.8 us
    pallas_call x1, Pallas kernels, body(): pl.pallas_call(front_kernel, out_shape=jax.ShapeDtypeStruct((OWN_DEV, wid...  9.69 us
    all_to_all x1, waiting for transfers between devices, body(): lax.all_to_all(total.reshape(n, 32, 128), 'dev', split_axis=0, concat_axi...  9.65 us
    pallas_call x1, Pallas kernels, body(): pl.pallas_call(grads_kernel, out_shape=(pltpu.HBM((t, width), BF), pltpu....  6.37 us
    all_to_all x1, starting transfers between devices, body(): lax.all_to_all(total.reshape(n, 32, 128), 'dev', split_axis=0, concat_axi...  4.6 us
    pallas_call x2, Pallas kernels, body(): pl.pallas_call(functools.partial(fill_kernel, scale, mine_too), out_shape...  2.82 us
    pallas_call x1, Pallas kernels, body(): pl.pallas_call(reduce_kernel, out_shape=pltpu.HBM((n // 2, 2, 32, 128), B...  2.29 us
    pallas_call x1, Pallas kernels, body(): pl.pallas_call(pack_kernel, out_shape=pltpu.VMEM((n, CHUNK, 128), BF), in...  2.08 us
  transfers between devices with their start and end apart: 3, of which 3 were waited for; matrix products, arithmetic and copies ran while one was open for 0% of the time, Pallas kernels for 13%

profile of v2, /device:TPU:1, one launch (start us, length us, event | category | flops | bytes accessed | tf_op | source)
XLA Modules:
  0.0 99.7 jit_solution(387729973885608232)
XLA Ops:
  0.6 6.4 %grads.1 = (bf16[512,512]{1,0:T(8,128)(2,1)}, bf16[512,512]{1,0:T(8,128)(2,1)S(1)}, bf16[1024,512]{1,0:T(8,128)(2,1)S(1)}, bf16[1024,512]{1,0:T(8,128)(2,1)S(1)}...) custom-call(s32[1]{0:T(128)} %bitcast.me, bf16[512,512]{1,0:T(8,128)(2,1)} %h_in.1, bf16[512,512]{1,0:T(8,128)(2,1)} %a_in.1, ...), custom_call_target="tpu_custom_call" | custom-call | tf_op jit(solution)/shard_map/grads/pallas_call | solution.py:318
  7.0 1.5 %collective-permute-start = (bf16[1024,512]{1,0:T(8,128)(2,1)S(1)}, bf16[1024,512]{1,0:T(8,128)(2,1)S(1)}, u32[]{:S(2)}, u32[]{:S(2)}) collective-permute-start(bf16[1024,512]{1,0:T(8,128)(2,1)S(1)} %get-tuple-element.21), channel_id=1, source_target_pairs={{0,1},{1,0},{2,3},{3,2},{4,5},{5,4},{6,7},{7,6},{8,9},{9,8},{10,11... | collective-permute-start | bytes 3145736 | tf_op jit(solution)/shard_map/core_exchange/ppermute | solution.py:342
  8.5 2.1 %pack.1 = bf16[128,112,128]{2,1,0:T(8,128)(2,1)S(1)} custom-call(s32[8,512]{1,0:T(8,128)S(1)} %get-tuple-element.22.places, bf16[4,128,128]{2,1,0:T(8,128)(2,1)S(1)} %get-tuple-element.23.kinds, bf16[512,512]{1,0:T(8,128)(2,1)S(1)} %get-tuple-element.24.message), custom_call_target="tpu_custom_call" | custom-call | tf_op jit(solution)/shard_map/pack/pallas_call | solution.py:344
  10.6 0.2 collective-permute-done.got
  10.8 0.3 join.1
  11.1 57.8 %all_to_all.10.received = bf16[128,112,128]{2,1,0:T(8,128)(2,1)} all-to-all(bf16[128,112,128]{2,1,0:T(8,128)(2,1)S(1)} %bitcast.11), channel_id=1, replica_groups=mesh['dev'=128] {'dev'}, dimensions={0} | all-to-all | bytes 7340032 | tf_op jit(solution)/shard_map/rows_to_owners/all_to_all | solution.py:361
  68.9 2.3 %sum_parts.1 = bf16[64,2,32,128]{3,2,1,0:T(8,128)(2,1)} custom-call(bf16[64,2,112,128]{3,2,1,0:T(8,128)(2,1)} %bitcast.14), custom_call_target="tpu_custom_call" | custom-call | tf_op jit(solution)/shard_map/sum_parts/pallas_call | solution.py:365
  71.2 4.6 %all-to-all-start.1 = ((bf16[128,32,128]{2,1,0:T(8,128)(2,1)}), bf16[128,32,128]{2,1,0:T(8,128)(2,1)S(1)}, u32[]{:S(2)}, u32[]{:S(2)}) async-start(bf16[128,32,128]{2,1,0:T(8,128)(2,1)} %bitcast.15), calls=%async_computation.1 | async-start | bytes 2097152 | tf_op jit(solution)/shard_map/sums_to_all/all_to_all | solution.py:379
  75.8 9.7 %front.1 = f32[2048,512]{1,0:T(8,128)} custom-call(bf16[128,112,128]{2,1,0:T(8,128)(2,1)} %all_to_all.10.received), custom_call_target="tpu_custom_call" | custom-call | flops 4831838208 | bytes 8388608 | tf_op jit(solution)/shard_map/front/pallas_call | solution.py:383
  85.5 9.7 %all-to-all-done.1 = bf16[128,32,128]{2,1,0:T(8,128)(2,1)S(1)} async-done(((bf16[128,32,128]{2,1,0:T(8,128)(2,1)}), bf16[128,32,128]{2,1,0:T(8,128)(2,1)S(1)}, u32[]{:S(2)}, u32[]{:S(2)}) %all-to-all-start.1) | async-done | bytes 1048608 | tf_op jit(solution)/shard_map/sums_to_all/all_to_all | solution.py:379
  95.1 0.9 collective-permute-start.1
  96.0 1.4 %fill_own.1 = (f32[1024,512]{1,0:T(8,128)}, f32[512,512]{1,0:T(8,128)}, f32[512,512]{1,0:T(8,128)}) custom-call(s32[1]{0:T(128)} %bitcast.me, bf16[64,2,32,128]{3,2,1,0:T(8,128)(2,1)S(1)} %bitcast.12), custom_call_target="tpu_custom_call" | custom-call | flops 524288 | bytes 3145728 | tf_op jit(solution)/shard_map/fill_own/pallas_call | solution.py:405
  97.4 0.9 collective-permute-done.1
  98.3 1.4 %fill_other.1 = (f32[1024,512]{1,0:T(8,128)}, f32[512,512]{1,0:T(8,128)}, f32[512,512]{1,0:T(8,128)}) custom-call(s32[1]{0:T(128)} %bitcast.me, bf16[64,2,32,128]{3,2,1,0:T(8,128)(2,1)S(1)} %bitcast.13, f32[1024,512]{1,0:T(8,128)} %get-tuple-element.27.refs_0_, ...), custom_call_target="tpu_custom_call", output_to_operand_aliasing={{0}: (2, {}), {1}: (3, {}), {2}: (4, {})} | custom-call | flops 524288 | bytes 3145728 | tf_op jit(solution)/shard_map/fill_other/pallas_call | solution.py:405
Async XLA Ops:
  7.0 3.8 %collective-permute-start = (bf16[1024,512]{1,0:T(8,128)(2,1)S(1)}, bf16[1024,512]{1,0:T(8,128)(2,1)S(1)}, u32[]{:S(2)}, u32[]{:S(2)}) collective-permute-start(bf16[1024,512]{1,0:T(8,128)(2,1)S(1)} %get-tuple-element.21), channel_id=1, source_target_pairs={{0,1},{1,0},{2,3},{3,2},{4,5},{5,4},{6,7},{7,6},{8,9},{9,8},{10,11... | collective-permute-start | bytes 3145736 | tf_op jit(solution)/shard_map/core_exchange/ppermute | solution.py:342
  71.2 23.9 %all-to-all-start.1 = ((bf16[128,32,128]{2,1,0:T(8,128)(2,1)}), bf16[128,32,128]{2,1,0:T(8,128)(2,1)S(1)}, u32[]{:S(2)}, u32[]{:S(2)}) async-start(bf16[128,32,128]{2,1,0:T(8,128)(2,1)} %bitcast.15), calls=%async_computation.1 | async-start | bytes 2097152 | tf_op jit(solution)/shard_map/sums_to_all/all_to_all | solution.py:379
  95.1 3.2 %collective-permute-start.1 = (bf16[128,32,128]{2,1,0:T(8,128)(2,1)S(1)}, bf16[128,32,128]{2,1,0:T(8,128)(2,1)S(1)}, u32[]{:S(2)}, u32[]{:S(2)}) collective-permute-start(bf16[128,32,128]{2,1,0:T(8,128)(2,1)S(1)} %all-to-all-done.1), channel_id=1, source_target_pairs={{0,1},{1,0},{2,3},{3,2},{4,5},{5,4},{6,7},{7,6},{8,9},{9,8},{10,11... | collective-permute-start | bytes 3145736 | tf_op jit(solution)/shard_map/core_exchange_back/ppermute | solution.py:400

commit v3 on v2

--- a/solution.py
+++ b/solution.py
@@ -20,6 +20,7 @@
 BF = jnp.bfloat16
 F32 = jnp.float32
 I32 = jnp.int32
+I16 = jnp.int16
 
 
 def mm(a, b):
@@ -35,38 +36,40 @@
 
 
 def onehot(flag):
-    return jnp.where(flag, 1.0, 0.0).astype(BF)
-
-
-def slot_kinds(me, slot, named, ranks):
-    t = named[0].shape[1]
-    lane = lax.broadcasted_iota(I32, (256, t), 0)
-    at_main = (me % 8) * MAIN
-    at_rest = (me % 64) * REST - MAIN + 128
-    values, lanes = [], []
+    return jnp.where(flag, jnp.ones((), BF), jnp.zeros((), BF))
+
+
+def slot_kinds(me, slot, hots, ranks):
+    t = slot.shape[1]
+    row = lax.broadcasted_iota(I32, (32, t), 0)
+    values = []
     for j, rank in enumerate(ranks):
-        value = slot[j]
-        high, low = (value // 64).astype(F32), (value % 64).astype(F32)
-        values.append(
-            jnp.concatenate(
-                [jnp.where(named[j], high, 0.0), jnp.where(named[j], low, 0.0)], axis=0
-            ).astype(BF)
-        )
-        lanes.append(onehot(lane == rank + jnp.where(rank < MAIN, at_main, at_rest)))
-    return mm_nt(jnp.concatenate(values, axis=1), jnp.concatenate(lanes, axis=1))
+        value = slot[j : j + 1, :]
+        at = row == rank
+        high = jnp.where(at, (value // 64).astype(F32), 0.0)
+        low = jnp.where(at, (value % 64).astype(F32), 0.0)
+        values.append(jnp.concatenate([high, low], axis=0).astype(BF))
+    by_rank = mm_nt(jnp.concatenate(hots, axis=1), jnp.concatenate(values, axis=1)).astype(BF)
+    source = lax.broadcasted_iota(I32, (64, 512), 0)
+    target = lax.broadcasted_iota(I32, (64, 512), 1)
+    rank, part = source % 32, source // 32
+    in_main = rank < MAIN
+    lane = jnp.where(in_main, (me % 8) * MAIN + rank, (me % 64) * REST + rank - MAIN)
+    kind = jnp.where(in_main, 0, 2) + part
+    return mm(by_rank, onehot((rank < CAP) & (target == kind * 128 + lane)))
 
 
 def grads_kernel(
-    me, h_in, a_in, go_in, ws_in, wn_in, owner_in, slot_in, hub_in,
-    grad_self, message, mine, send, places, kinds,
-    h, a, go, ws, wn, owner, slot, hub, back, arrived,
+    me, h_in, a_in, go_in, ws_in, wn_in, hub_in, owner_in, slot_in,
+    grad_self, message, mine, send, owner, slot,
+    h, a, go, ws, wn, hub, back, arrived,
 ):
     loads = [
         pltpu.make_async_copy(src, dst, arrived.at[i])
         for i, (src, dst) in enumerate(
             (
-                (owner_in, owner), (slot_in, slot), (hub_in, hub),
-                (h_in, h), (ws_in, ws), (a_in, a), (wn_in, wn), (go_in, go),
+                (h_in, h), (ws_in, ws), (a_in, a), (wn_in, wn), (go_in, go), (hub_in, hub),
+                (owner_in, owner), (slot_in, slot),
             )
         )
     ]
@@ -74,15 +77,70 @@
         load.start()
 
     t = h.shape[0]
-    n = kinds.shape[1]
+    loads[0].wait()
+    loads[1].wait()
+    pre = mm(h[...], ws[...])
+    loads[2].wait()
+    loads[3].wait()
+    pre = pre + mm(a[...], wn[...])
+    loads[4].wait()
+    sig = jax.nn.sigmoid(pre)
+    g = (go[...].astype(F32) * (sig * (1.0 + pre * (1.0 - sig)))).astype(BF)
+    back[...] = mm_nt(g, ws[...]).astype(BF)
+    store = pltpu.make_async_copy(back, grad_self, arrived.at[8])
+    store.start()
+    msg = (mm_nt(g, wn[...]) / FANOUT).astype(BF)
+    message[...] = msg
+    loads[5].wait()
+    rows = lax.broadcasted_iota(I16, (HUBS, t), 0)
+    ids = hub[...].astype(I16)
+    count = onehot(rows == ids[0:1, :]) + onehot(rows == ids[1:2, :])
+    hub_part = mm(count, msg).astype(BF)
+    depth = h.shape[1]
+    first = lax.rem(me[0], 2) == 0
+    part_self = mm_tn(h[...], g).astype(BF)
+    part_neigh = mm_tn(a[...], g).astype(BF)
+
+    @pl.when(first)
+    def _():
+        mine[...] = hub_part
+        send[0:depth, :] = part_self
+        send[depth : 2 * depth, :] = part_neigh
+
+    @pl.when(jnp.logical_not(first))
+    def _():
+        send[...] = hub_part
+        mine[0:depth, :] = part_self
+        mine[depth : 2 * depth, :] = part_neigh
+
+    store.wait()
+    loads[6].wait()
+    loads[7].wait()
+
+
+def spread_rows():
+    row = lax.broadcasted_iota(I32, (GROUP * 16, 192), 0)
+    col = lax.broadcasted_iota(I32, (GROUP * 16, 192), 1)
+    chunk, s = row // 16, row % 16
+    want = jnp.where(s < 8, (s // 2) * 32 + chunk * 2 + s % 2, 128 + (s - 8) * 16 + chunk)
+    return onehot((s < 12) & (col == want))
+
+
+def picks(places, at):
+    return onehot((at == places[0]) | (at == places[1]) | (at == places[2]))
+
+
+def pack_kernel(me, owner, slot, message, out):
+    t = message.shape[0]
+    n = out.shape[0]
     fan = slot.shape[0]
     device = lax.broadcasted_iota(I32, (n, t), 0)
-    before = onehot(lax.broadcasted_iota(I32, (t, t), 0) < lax.broadcasted_iota(I32, (t, t), 1))
-    loads[0].wait()
-    loads[1].wait()
+    before = onehot(
+        lax.broadcasted_iota(I16, (t, t), 0) < lax.broadcasted_iota(I16, (t, t), 1)
+    )
     named = [device == owner[j] for j in range(fan)]
-    slots = [slot[j : j + 1, :] for j in range(fan)]
-    hot = jnp.concatenate([onehot(f) for f in named], axis=0)
+    hots = [onehot(f) for f in named]
+    hot = jnp.concatenate(hots, axis=0)
     earlier = mm(hot, before)
     amount = jnp.sum(hot.astype(F32), axis=1, keepdims=True)
     base = jnp.zeros((n, 1), F32)
@@ -91,89 +149,28 @@
         rank = jnp.where(named[j], earlier[j * n : (j + 1) * n, :] + base, 0.0)
         ranks.append(jnp.sum(rank, axis=0, keepdims=True).astype(I32))
         base = base + amount[j * n : (j + 1) * n, :]
-    for j in range(fan):
-        in_main = ranks[j] < MAIN
-        places[j : j + 1, :] = jnp.where(in_main, owner[j] * MAIN + ranks[j], -1)
-        places[4 + j : 5 + j, :] = jnp.where(in_main, -1, owner[j] * REST + (ranks[j] - MAIN))
-    kind = slot_kinds(me[0], slots, named, ranks).astype(BF)
-    for i in range(4):
-        kinds[i] = kind[(i % 2) * n : (i % 2 + 1) * n, (i // 2) * 128 : (i // 2 + 1) * 128]
-    loads[2].wait()
-    rows = lax.broadcasted_iota(I32, (HUBS, t), 0)
-    count = onehot(rows == hub[0:1, :]) + onehot(rows == hub[1:2, :])
-
-    loads[3].wait()
-    loads[4].wait()
-    pre = mm(h[...], ws[...])
-    loads[5].wait()
-    loads[6].wait()
-    pre = pre + mm(a[...], wn[...])
-    loads[7].wait()
-    sig = jax.nn.sigmoid(pre)
-    g = (go[...].astype(F32) * (sig * (1.0 + pre * (1.0 - sig)))).astype(BF)
-    back[...] = mm_nt(g, ws[...]).astype(BF)
-    store = pltpu.make_async_copy(back, grad_self, arrived.at[8])
-    store.start()
-    msg = (mm_nt(g, wn[...]) / FANOUT).astype(BF)
-    message[...] = msg
-    hub_part = mm(count, msg).astype(BF)
-    depth = h.shape[1]
-    first = lax.rem(me[0], 2) == 0
-    part_self = mm_tn(h[...], g).astype(BF)
-    part_neigh = mm_tn(a[...], g).astype(BF)
-
-    @pl.when(first)
-    def _():
-        mine[...] = hub_part
-        send[0:depth, :] = part_self
-        send[depth : 2 * depth, :] = part_neigh
-
-    @pl.when(jnp.logical_not(first))
-    def _():
-        send[...] = hub_part
-        mine[0:depth, :] = part_self
-        mine[depth : 2 * depth, :] = part_neigh
-
-    store.wait()
-
-
-def spread_rows():
-    row = lax.broadcasted_iota(I32, (GROUP * 16, 192), 0)
-    col = lax.broadcasted_iota(I32, (GROUP * 16, 192), 1)
-    chunk, s = row // 16, row % 16
-    want = jnp.where(s < 8, (s // 2) * 32 + chunk * 2 + s % 2, 128 + (s - 8) * 16 + chunk)
-    return onehot((s < 12) & (col == want))
-
-
-def picks(places, first, at):
-    flag = at == places[first : first + 1, :]
-    for j in range(first + 1, first + 3):
-        flag = flag | (at == places[j : j + 1, :])
-    return onehot(flag)
-
-
-def pack_kernel(places, kinds, message, out):
-    t = message.shape[0]
-    chunks = out.shape[0]
+    main, last = [], []
+    for j, rank in enumerate(ranks):
+        in_main = rank < MAIN
+        main.append(jnp.where(in_main, owner[j] * MAIN + rank, -1).astype(I16))
+        last.append(jnp.where(in_main, -1, owner[j] * REST + (rank - MAIN)).astype(I16))
+    kinds = slot_kinds(me[0], slot[...], hots, ranks).astype(BF)
+
+    msg = message[...]
     spread = spread_rows()
-    msg = message[...]
-    at = lax.broadcasted_iota(I32, (chunks * MAIN, t), 0)
-    rows = mm(picks(places, 0, at), msg).astype(BF)
-    for q in range(4):
-        out[:, q * 16 : (q + 1) * 16, :] = rows[:, q * 128 : (q + 1) * 128].reshape(
-            chunks, 16, 128
-        )
-    at = lax.broadcasted_iota(I32, (chunks * REST, t), 0)
-    rest = mm(picks(places, 4, at), msg).astype(BF)
-    for g in range(chunks // GROUP):
+    rest = mm(picks(last, lax.broadcasted_iota(I16, (n * REST, t), 0)), msg).astype(BF)
+    for g in range(n // GROUP):
         stacked = jnp.concatenate(
             [rest[g * 32 : (g + 1) * 32, q * 128 : (q + 1) * 128] for q in range(4)]
-            + [kinds[i, g * GROUP : (g + 1) * GROUP, :] for i in range(4)],
+            + [kinds[g * GROUP : (g + 1) * GROUP, q * 128 : (q + 1) * 128] for q in range(4)],
             axis=0,
         )
         out[g * GROUP : (g + 1) * GROUP, 64:80, :] = (
             mm(spread, stacked).astype(BF).reshape(GROUP, 16, 128)
         )
+    rows = mm(picks(main, lax.broadcasted_iota(I16, (n * MAIN, t), 0)), msg).astype(BF)
+    for q in range(4):
+        out[:, q * 16 : (q + 1) * 16, :] = rows[:, q * 128 : (q + 1) * 128].reshape(n, 16, 128)
 
 
 def join_kernel(mine, got, held, out):
@@ -310,44 +307,39 @@
     slot_t = slot.T
     hub_t = hub_refs.T
     swap = [(i, i ^ 1) for i in range(n)]
-    half = jax.ShapeDtypeStruct((HUBS, width), BF)
-    same = jax.ShapeDtypeStruct((t, width), BF)
-
-    fan = slot.shape[1]
+
     with jax.named_scope("grads"):
-        grad_self, message, mine, send, places, kinds = pl.pallas_call(
+        grad_self, message, mine, send, owner_v, slot_v = pl.pallas_call(
             grads_kernel,
             out_shape=(
                 pltpu.HBM((t, width), BF),
                 pltpu.VMEM((t, width), BF),
                 pltpu.VMEM((HUBS, width), BF),
                 pltpu.VMEM((HUBS, width), BF),
-                pltpu.VMEM((8, t), I32),
-                pltpu.VMEM((4, n, 128), BF),
+                pltpu.VMEM(owner_t.shape, I32),
+                pltpu.VMEM(slot_t.shape, I32),
             ),
             in_specs=[SMEM] + [HBM] * 8,
             out_specs=[HBM] + [VMEM] * 5,
             scratch_shapes=[pltpu.VMEM((t, width), BF)] * 3
             + [pltpu.VMEM((width, width), BF)] * 2
             + [
-                pltpu.VMEM((fan, 1, t), I32),
-                pltpu.VMEM((fan, t), I32),
                 pltpu.VMEM(hub_t.shape, I32),
                 pltpu.VMEM((t, width), BF),
                 pltpu.SemaphoreType.DMA((9,)),
             ],
             compiler_params=PARAMS,
-        )(me, *map(in_hbm, (h_self, agg, grad_out, w_self, w_neigh, owner_t, slot_t, hub_t)))
+        )(me, *map(in_hbm, (h_self, agg, grad_out, w_self, w_neigh, hub_t, owner_t, slot_t)))
     with jax.named_scope("core_exchange"):
         got = lax.ppermute(send, "dev", swap)
     with jax.named_scope("pack"):
         packed = pl.pallas_call(
             pack_kernel,
             out_shape=pltpu.VMEM((n, CHUNK, 128), BF),
-            in_specs=[VMEM] * 3,
+            in_specs=[SMEM] + [VMEM] * 3,
             out_specs=VMEM,
             compiler_params=PARAMS,
-        )(*map(in_vmem, (places, kinds, message)))
+        )(me, *map(in_vmem, (owner_v, slot_v, message)))
     with jax.named_scope("join"):
         packed = pl.pallas_call(
             join_kernel,

time: 99.9 us -> 98.1 us (0.982)
  Pallas kernels: 23.5 us -> 22.1 us
    pallas_call x1, Pallas kernels: 6.37 us -> 4.55 us  [body(): pl.pallas_call(grads_kernel, out_shape=(pltpu.HBM((t, width), BF), pltpu....]
  transfers between devices with their start and end apart: 3 -> 3, of which waited for: 3 -> 2; matrix products, arithmetic and copies ran while one was open for 0% -> 0% of each run, Pallas kernels for 13% -> 14%
where the time goes in v3:
time: 98.1 us; the launch traced here: 97.9 us
  blocking collectives  57.6 us (59%)
  Pallas kernels  22.1 us (23%)
  waiting for transfers between devices  10.6 us (11%)
  starting transfers between devices  6.96 us (7%)
    all_to_all x1, blocking collectives, body(): lax.all_to_all(packed.reshape(n, CHUNK, 128), 'dev', split_axis=0, concat...  57.6 us
    all_to_all x1, waiting for transfers between devices, body(): lax.all_to_all(total.reshape(n, 32, 128), 'dev', split_axis=0, concat_axi...  9.68 us
    pallas_call x1, Pallas kernels, body(): pl.pallas_call(front_kernel, out_shape=jax.ShapeDtypeStruct((OWN_DEV, wid...  9.67 us
    all_to_all x1, starting transfers between devices, body(): lax.all_to_all(total.reshape(n, 32, 128), 'dev', split_axis=0, concat_axi...  4.6 us
    pallas_call x1, Pallas kernels, body(): pl.pallas_call(grads_kernel, out_shape=(pltpu.HBM((t, width), BF), pltpu....  4.55 us
    pallas_call x2, Pallas kernels, body(): pl.pallas_call(functools.partial(fill_kernel, scale, mine_too), out_shape...  2.82 us
    pallas_call x1, Pallas kernels, body(): pl.pallas_call(pack_kernel, out_shape=pltpu.VMEM((n, CHUNK, 128), BF), in...  2.49 us
    pallas_call x1, Pallas kernels, body(): pl.pallas_call(reduce_kernel, out_shape=pltpu.HBM((n // 2, 2, 32, 128), B...  2.29 us
  transfers between devices with their start and end apart: 3, of which 2 were waited for; matrix products, arithmetic and copies ran while one was open for 0% of the time, Pallas kernels for 14%

profile of v3, /device:TPU:1, one launch (start us, length us, event | category | flops | bytes accessed | tf_op | source)
XLA Modules:
  0.0 97.9 jit_solution(17526723038267801135)
XLA Ops:
  0.6 4.5 %grads.1 = (bf16[512,512]{1,0:T(8,128)(2,1)}, bf16[512,512]{1,0:T(8,128)(2,1)S(1)}, bf16[1024,512]{1,0:T(8,128)(2,1)S(1)}, bf16[1024,512]{1,0:T(8,128)(2,1)S(1)}...) custom-call(s32[1]{0:T(128)} %bitcast.me, bf16[512,512]{1,0:T(8,128)(2,1)} %h_in.1, bf16[512,512]{1,0:T(8,128)(2,1)} %a_in.1, ...), custom_call_target="tpu_custom_call" | custom-call | tf_op jit(solution)/shard_map/grads/pallas_call | solution.py:312
  5.2 1.5 %collective-permute-start = (bf16[1024,512]{1,0:T(8,128)(2,1)S(1)}, bf16[1024,512]{1,0:T(8,128)(2,1)S(1)}, u32[]{:S(2)}, u32[]{:S(2)}) collective-permute-start(bf16[1024,512]{1,0:T(8,128)(2,1)S(1)} %get-tuple-element.21), channel_id=1, source_target_pairs={{0,1},{1,0},{2,3},{3,2},{4,5},{5,4},{6,7},{7,6},{8,9},{9,8},{10,11... | collective-permute-start | bytes 3145736 | tf_op jit(solution)/shard_map/core_exchange/ppermute | solution.py:334
  6.7 2.5 %pack.1 = bf16[128,112,128]{2,1,0:T(8,128)(2,1)S(1)} custom-call(s32[1]{0:T(128)} %bitcast.me, s32[3,1,512]{2,1,0:T(1,128)S(1)} %get-tuple-element.22.owner, s32[3,512]{1,0:T(4,128)S(1)} %get-tuple-element.23.slot, bf16[512,512]{1,0:T(8,128)(2,1)S(1)} %get-tuple-element.24.message), custom_call_target="tpu_custom_call" | custom-call | tf_op jit(solution)/shard_map/pack/pallas_call | solution.py:336
  9.2 0.0 collective-permute-done.got
  9.2 0.3 join.1
  9.5 57.6 %all_to_all.10.received = bf16[128,112,128]{2,1,0:T(8,128)(2,1)} all-to-all(bf16[128,112,128]{2,1,0:T(8,128)(2,1)S(1)} %bitcast.11), channel_id=1, replica_groups=mesh['dev'=128] {'dev'}, dimensions={0} | all-to-all | bytes 7340032 | tf_op jit(solution)/shard_map/rows_to_owners/all_to_all | solution.py:353
  67.0 2.3 %sum_parts.1 = bf16[64,2,32,128]{3,2,1,0:T(8,128)(2,1)} custom-call(bf16[64,2,112,128]{3,2,1,0:T(8,128)(2,1)} %bitcast.14), custom_call_target="tpu_custom_call" | custom-call | tf_op jit(solution)/shard_map/sum_parts/pallas_call | solution.py:357
  69.3 4.6 %all-to-all-start.1 = ((bf16[128,32,128]{2,1,0:T(8,128)(2,1)}), bf16[128,32,128]{2,1,0:T(8,128)(2,1)S(1)}, u32[]{:S(2)}, u32[]{:S(2)}) async-start(bf16[128,32,128]{2,1,0:T(8,128)(2,1)} %bitcast.15), calls=%async_computation.1 | async-start | bytes 2097152 | tf_op jit(solution)/shard_map/sums_to_all/all_to_all | solution.py:371
  74.0 9.7 %front.1 = f32[2048,512]{1,0:T(8,128)} custom-call(bf16[128,112,128]{2,1,0:T(8,128)(2,1)} %all_to_all.10.received), custom_call_target="tpu_custom_call" | custom-call | flops 4831838208 | bytes 8388608 | tf_op jit(solution)/shard_map/front/pallas_call | solution.py:375
  83.6 9.7 %all-to-all-done.1 = bf16[128,32,128]{2,1,0:T(8,128)(2,1)S(1)} async-done(((bf16[128,32,128]{2,1,0:T(8,128)(2,1)}), bf16[128,32,128]{2,1,0:T(8,128)(2,1)S(1)}, u32[]{:S(2)}, u32[]{:S(2)}) %all-to-all-start.1) | async-done | bytes 1048608 | tf_op jit(solution)/shard_map/sums_to_all/all_to_all | solution.py:371
  93.3 0.9 collective-permute-start.1
  94.2 1.4 %fill_own.1 = (f32[1024,512]{1,0:T(8,128)}, f32[512,512]{1,0:T(8,128)}, f32[512,512]{1,0:T(8,128)}) custom-call(s32[1]{0:T(128)} %bitcast.me, bf16[64,2,32,128]{3,2,1,0:T(8,128)(2,1)S(1)} %bitcast.12), custom_call_target="tpu_custom_call" | custom-call | flops 524288 | bytes 3145728 | tf_op jit(solution)/shard_map/fill_own/pallas_call | solution.py:397
  95.6 0.9 collective-permute-done.1
  96.5 1.4 %fill_other.1 = (f32[1024,512]{1,0:T(8,128)}, f32[512,512]{1,0:T(8,128)}, f32[512,512]{1,0:T(8,128)}) custom-call(s32[1]{0:T(128)} %bitcast.me, bf16[64,2,32,128]{3,2,1,0:T(8,128)(2,1)S(1)} %bitcast.13, f32[1024,512]{1,0:T(8,128)} %get-tuple-element.27.refs_0_, ...), custom_call_target="tpu_custom_call", output_to_operand_aliasing={{0}: (2, {}), {1}: (3, {}), {2}: (4, {})} | custom-call | flops 524288 | bytes 3145728 | tf_op jit(solution)/shard_map/fill_other/pallas_call | solution.py:397
Async XLA Ops:
  5.2 4.0 %collective-permute-start = (bf16[1024,512]{1,0:T(8,128)(2,1)S(1)}, bf16[1024,512]{1,0:T(8,128)(2,1)S(1)}, u32[]{:S(2)}, u32[]{:S(2)}) collective-permute-start(bf16[1024,512]{1,0:T(8,128)(2,1)S(1)} %get-tuple-element.21), channel_id=1, source_target_pairs={{0,1},{1,0},{2,3},{3,2},{4,5},{5,4},{6,7},{7,6},{8,9},{9,8},{10,11... | collective-permute-start | bytes 3145736 | tf_op jit(solution)/shard_map/core_exchange/ppermute | solution.py:334
  69.3 23.9 %all-to-all-start.1 = ((bf16[128,32,128]{2,1,0:T(8,128)(2,1)}), bf16[128,32,128]{2,1,0:T(8,128)(2,1)S(1)}, u32[]{:S(2)}, u32[]{:S(2)}) async-start(bf16[128,32,128]{2,1,0:T(8,128)(2,1)} %bitcast.15), calls=%async_computation.1 | async-start | bytes 2097152 | tf_op jit(solution)/shard_map/sums_to_all/all_to_all | solution.py:371
  93.3 3.2 %collective-permute-start.1 = (bf16[128,32,128]{2,1,0:T(8,128)(2,1)S(1)}, bf16[128,32,128]{2,1,0:T(8,128)(2,1)S(1)}, u32[]{:S(2)}, u32[]{:S(2)}) collective-permute-start(bf16[128,32,128]{2,1,0:T(8,128)(2,1)S(1)} %all-to-all-done.1), channel_id=1, source_target_pairs={{0,1},{1,0},{2,3},{3,2},{4,5},{5,4},{6,7},{7,6},{8,9},{9,8},{10,11... | collective-permute-start | bytes 3145736 | tf_op jit(solution)/shard_map/core_exchange_back/ppermute | solution.py:392

commit v4 on v3

--- a/solution.py
+++ b/solution.py
@@ -61,8 +61,8 @@
 
 def grads_kernel(
     me, h_in, a_in, go_in, ws_in, wn_in, hub_in, owner_in, slot_in,
-    grad_self, message, mine, send, owner, slot,
-    h, a, go, ws, wn, hub, back, arrived,
+    g_out, message, mine, send, owner, slot,
+    h, a, go, ws, wn, hub, g, arrived,
 ):
     loads = [
         pltpu.make_async_copy(src, dst, arrived.at[i])
@@ -85,11 +85,10 @@
     pre = pre + mm(a[...], wn[...])
     loads[4].wait()
     sig = jax.nn.sigmoid(pre)
-    g = (go[...].astype(F32) * (sig * (1.0 + pre * (1.0 - sig)))).astype(BF)
-    back[...] = mm_nt(g, ws[...]).astype(BF)
-    store = pltpu.make_async_copy(back, grad_self, arrived.at[8])
+    g[...] = (go[...].astype(F32) * (sig * (1.0 + pre * (1.0 - sig)))).astype(BF)
+    store = pltpu.make_async_copy(g, g_out, arrived.at[8])
     store.start()
-    msg = (mm_nt(g, wn[...]) / FANOUT).astype(BF)
+    msg = (mm_nt(g[...], wn[...]) / FANOUT).astype(BF)
     message[...] = msg
     loads[5].wait()
     rows = lax.broadcasted_iota(I16, (HUBS, t), 0)
@@ -98,8 +97,8 @@
     hub_part = mm(count, msg).astype(BF)
     depth = h.shape[1]
     first = lax.rem(me[0], 2) == 0
-    part_self = mm_tn(h[...], g).astype(BF)
-    part_neigh = mm_tn(a[...], g).astype(BF)
+    part_self = mm_tn(h[...], g[...]).astype(BF)
+    part_neigh = mm_tn(a[...], g[...]).astype(BF)
 
     @pl.when(first)
     def _():
@@ -182,39 +181,27 @@
             out[:, half, first : first + 16, :] = total.astype(BF).reshape(-1, 16, 128)
 
 
-def reduce_kernel(received, out, parts, total, arrived, left):
-    chips = parts.shape[0]
-    steps, copies = arrived.shape[0], left.shape[0]
-    piece, each = chips // steps, total.shape[0]
-    loads = [
-        pltpu.make_async_copy(
-            received.at[pl.ds(i * piece, piece), :, pl.ds(FRONT, 32), :],
-            parts.at[pl.ds(i * piece, piece)],
-            arrived.at[i],
-        )
-        for i in range(steps)
+def reduce_kernel(received, out, kept, total, left):
+    chips, each = received.shape[0], total.shape[0]
+    acc = jnp.sum(received[:, :, FRONT : FRONT + 32, :].astype(F32), axis=0, keepdims=True)
+    total[...] = jnp.broadcast_to(acc.astype(BF), total.shape)
+    copies = [
+        pltpu.make_async_copy(total, out.at[pl.ds(i * each, each)], left.at[1 + i])
+        for i in range(chips // each)
     ]
-    for load in loads:
-        load.start()
-    acc = jnp.zeros((1, 2, 32, 128), F32)
-    for i, load in enumerate(loads):
-        load.wait()
-        block = parts[i * piece : (i + 1) * piece].astype(F32)
-        acc = acc + jnp.sum(block, axis=0, keepdims=True)
-    total[...] = jnp.broadcast_to(acc.astype(BF), total.shape)
-    stores = [
-        pltpu.make_async_copy(total, out.at[pl.ds(i * each, each)], left.at[i])
-        for i in range(copies)
-    ]
-    for store in stores:
-        store.start()
-    for store in stores:
-        store.wait()
-
-
-def front_kernel(received, out, rows, index):
+    copies.append(
+        pltpu.make_async_copy(received.at[:, :, pl.ds(0, FRONT), :], kept, left.at[0])
+    )
+    for copy in copies:
+        copy.start()
+    for copy in copies:
+        copy.wait()
+
+
+def front_kernel(received, g, ws, out, grad_self, rows, index):
     step = pl.program_id(0)
     n = received.shape[0]
+    grad_self[...] = mm_nt(g[...], ws[...]).astype(BF)
 
     @pl.when(step == 0)
     def _():
@@ -309,7 +296,7 @@
     swap = [(i, i ^ 1) for i in range(n)]
 
     with jax.named_scope("grads"):
-        grad_self, message, mine, send, owner_v, slot_v = pl.pallas_call(
+        g, message, mine, send, owner_v, slot_v = pl.pallas_call(
             grads_kernel,
             out_shape=(
                 pltpu.HBM((t, width), BF),
@@ -354,30 +341,42 @@
             packed.reshape(n, CHUNK, 128), "dev", split_axis=0, concat_axis=0, tiled=True
         )
     with jax.named_scope("sum_parts"):
-        total = pl.pallas_call(
+        total, kept = pl.pallas_call(
             reduce_kernel,
-            out_shape=pltpu.HBM((n // 2, 2, 32, 128), BF),
-            in_specs=[HBM],
-            out_specs=HBM,
+            out_shape=(
+                pltpu.HBM((n // 2, 2, 32, 128), BF),
+                pltpu.HBM((n // 2, 2, FRONT, 128), BF),
+            ),
+            in_specs=[VMEM],
+            out_specs=[HBM] * 2,
             scratch_shapes=[
-                pltpu.VMEM((n // 2, 2, 32, 128), BF),
                 pltpu.VMEM((8, 2, 32, 128), BF),
-                pltpu.SemaphoreType.DMA((4,)),
-                pltpu.SemaphoreType.DMA((n // 16,)),
+                pltpu.SemaphoreType.DMA((1 + n // 16,)),
             ],
             compiler_params=PARAMS,
-        )(in_hbm(received.reshape(n // 2, 2, CHUNK, 128)))
+        )(in_vmem(received.reshape(n // 2, 2, CHUNK, 128)))
+        kept = kept.reshape(n, FRONT, 128)
     with jax.named_scope("sums_to_all"):
         own = lax.all_to_all(
             total.reshape(n, 32, 128), "dev", split_axis=0, concat_axis=0, tiled=True
         )
     with jax.named_scope("front"):
-        front_grad = pl.pallas_call(
+        front_grad, grad_self = pl.pallas_call(
             front_kernel,
-            out_shape=jax.ShapeDtypeStruct((OWN_DEV, width), F32),
+            out_shape=(
+                jax.ShapeDtypeStruct((OWN_DEV, width), F32),
+                jax.ShapeDtypeStruct((t, width), BF),
+            ),
             grid=(8,),
-            in_specs=[pl.BlockSpec((n, FRONT, 128), lambda i: (0, 0, 0))],
-            out_specs=pl.BlockSpec((OWN_DEV // 8, width), lambda i: (i, 0)),
+            in_specs=[
+                pl.BlockSpec((n, FRONT, 128), lambda i: (0, 0, 0)),
+                pl.BlockSpec((t // 8, width), lambda i: (i, 0)),
+                pl.BlockSpec((width, width), lambda i: (0, 0)),
+            ],
+            out_specs=(
+                pl.BlockSpec((OWN_DEV // 8, width), lambda i: (i, 0)),
+                pl.BlockSpec((t // 8, width), lambda i: (i, 0)),
+            ),
             scratch_shapes=[
                 pltpu.VMEM((n * CAP, width), BF),
                 pltpu.VMEM((24, 128), I32),
@@ -386,7 +385,7 @@
             cost_estimate=pl.CostEstimate(
                 flops=2 * OWN_DEV * n * CAP * width, bytes_accessed=8 << 20, transcendentals=0
             ),
-        )(in_hbm(received))
+        )(in_hbm(kept), in_hbm(g), in_hbm(w_self))
     own, front_grad = lax.optimization_barrier((own, front_grad))
     with jax.named_scope("core_exchange_back"):
         other = lax.ppermute(own, "dev", swap)

time: 98.1 us -> 97.5 us (level)
  waiting for transfers between devices: 10.6 us -> 8.18 us
  Pallas kernels: 22.1 us -> 24 us
    all_to_all x1, waiting for transfers between devices: 9.68 us -> 7.3 us  [body(): lax.all_to_all(total.reshape(n, 32, 128), 'dev', split_axis=0, concat_axi...]
    pallas_call x2, Pallas kernels: 12 us -> 14.1 us  [the longest x1 12 us: body(): pl.pallas_call(front_kernel, out_shape=(jax.ShapeDtypeStruct((OWN_DEV, wi...]
  transfers between devices with their start and end apart: 3 -> 3, of which waited for: 2 -> 2; matrix products, arithmetic and copies ran while one was open for 0% -> 0% of each run, Pallas kernels for 14% -> 16%
where the time goes in v4:
time: 97.5 us; the launch traced here: 97.3 us
  blocking collectives  57.5 us (59%)
  Pallas kernels  24 us (25%)
  waiting for transfers between devices  8.18 us (8%)
  starting transfers between devices  6.99 us (7%)
    all_to_all x1, blocking collectives, body(): lax.all_to_all(packed.reshape(n, CHUNK, 128), 'dev', split_axis=0, concat...  57.5 us
    pallas_call x1, Pallas kernels, body(): pl.pallas_call(front_kernel, out_shape=(jax.ShapeDtypeStruct((OWN_DEV, wi...  12 us
    all_to_all x1, waiting for transfers between devices, body(): lax.all_to_all(total.reshape(n, 32, 128), 'dev', split_axis=0, concat_axi...  7.3 us
    all_to_all x1, starting transfers between devices, body(): lax.all_to_all(total.reshape(n, 32, 128), 'dev', split_axis=0, concat_axi...  4.6 us
    pallas_call x1, Pallas kernels, body(): pl.pallas_call(grads_kernel, out_shape=(pltpu.HBM((t, width), BF), pltpu....  4.26 us
    pallas_call x2, Pallas kernels, body(): pl.pallas_call(functools.partial(fill_kernel, scale, mine_too), out_shape...  2.82 us
    pallas_call x1, Pallas kernels, body(): pl.pallas_call(pack_kernel, out_shape=pltpu.VMEM((n, CHUNK, 128), BF), in...  2.49 us
    pallas_call x1, Pallas kernels, body(): pl.pallas_call(reduce_kernel, out_shape=(pltpu.HBM((n // 2, 2, 32, 128),...  2.1 us
  transfers between devices with their start and end apart: 3, of which 2 were waited for; matrix products, arithmetic and copies ran while one was open for 0% of the time, Pallas kernels for 16%

profile of v4, /device:TPU:1, one launch (start us, length us, event | category | flops | bytes accessed | tf_op | source)
XLA Modules:
  0.0 97.3 jit_solution(15269173133223051995)
XLA Ops:
  0.6 4.3 %grads.1 = (bf16[512,512]{1,0:T(8,128)(2,1)}, bf16[512,512]{1,0:T(8,128)(2,1)S(1)}, bf16[1024,512]{1,0:T(8,128)(2,1)S(1)}, bf16[1024,512]{1,0:T(8,128)(2,1)S(1)}...) custom-call(s32[1]{0:T(128)} %bitcast.me, bf16[512,512]{1,0:T(8,128)(2,1)} %h_in.1, bf16[512,512]{1,0:T(8,128)(2,1)} %a_in.1, ...), custom_call_target="tpu_custom_call" | custom-call | tf_op jit(solution)/shard_map/grads/pallas_call | solution.py:299
  4.9 1.5 %collective-permute-start = (bf16[1024,512]{1,0:T(8,128)(2,1)S(1)}, bf16[1024,512]{1,0:T(8,128)(2,1)S(1)}, u32[]{:S(2)}, u32[]{:S(2)}) collective-permute-start(bf16[1024,512]{1,0:T(8,128)(2,1)S(1)} %get-tuple-element.24), channel_id=1, source_target_pairs={{0,1},{1,0},{2,3},{3,2},{4,5},{5,4},{6,7},{7,6},{8,9},{9,8},{10,11... | collective-permute-start | bytes 3145736 | tf_op jit(solution)/shard_map/core_exchange/ppermute | solution.py:321
  6.4 2.5 %pack.1 = bf16[128,112,128]{2,1,0:T(8,128)(2,1)S(1)} custom-call(s32[1]{0:T(128)} %bitcast.me, s32[3,1,512]{2,1,0:T(1,128)S(1)} %get-tuple-element.25.owner, s32[3,512]{1,0:T(4,128)S(1)} %get-tuple-element.26.slot, bf16[512,512]{1,0:T(8,128)(2,1)S(1)} %get-tuple-element.27.message), custom_call_target="tpu_custom_call" | custom-call | tf_op jit(solution)/shard_map/pack/pallas_call | solution.py:323
  8.9 0.0 collective-permute-done.got
  8.9 0.3 join.1
  9.2 57.5 %all_to_all.10 = bf16[128,112,128]{2,1,0:T(8,128)(2,1)S(1)} all-to-all(bf16[128,112,128]{2,1,0:T(8,128)(2,1)S(1)} %bitcast.12), channel_id=1, replica_groups=mesh['dev'=128] {'dev'}, dimensions={0} | all-to-all | bytes 7340032 | tf_op jit(solution)/shard_map/rows_to_owners/all_to_all | solution.py:340
  66.7 2.1 %sum_parts.1 = (bf16[64,2,32,128]{3,2,1,0:T(8,128)(2,1)}, bf16[64,2,80,128]{3,2,1,0:T(8,128)(2,1)}) custom-call(bf16[64,2,112,128]{3,2,1,0:T(8,128)(2,1)S(1)} %bitcast.13), custom_call_target="tpu_custom_call" | custom-call | tf_op jit(solution)/shard_map/sum_parts/pallas_call | solution.py:344
  68.8 4.6 %all-to-all-start.1 = ((bf16[128,32,128]{2,1,0:T(8,128)(2,1)}), bf16[128,32,128]{2,1,0:T(8,128)(2,1)S(1)}, u32[]{:S(2)}, u32[]{:S(2)}) async-start(bf16[128,32,128]{2,1,0:T(8,128)(2,1)} %bitcast.16), calls=%async_computation.1 | async-start | bytes 2097152 | tf_op jit(solution)/shard_map/sums_to_all/all_to_all | solution.py:360
  73.4 12.0 %front.1 = (f32[2048,512]{1,0:T(8,128)}, bf16[512,512]{1,0:T(8,128)(2,1)}) custom-call(bf16[128,80,128]{2,1,0:T(8,128)(2,1)} %bitcast.20, bf16[512,512]{1,0:T(8,128)(2,1)} %get-tuple-element.29.g, bf16[512,512]{1,0:T(8,128)(2,1)} %ws.1), custom_call_target="tpu_custom_call" | custom-call | flops 4831838208 | bytes 8388608 | tf_op jit(solution)/shard_map/front/pallas_call | solution.py:364
  85.4 7.3 %all-to-all-done.1 = bf16[128,32,128]{2,1,0:T(8,128)(2,1)S(1)} async-done(((bf16[128,32,128]{2,1,0:T(8,128)(2,1)}), bf16[128,32,128]{2,1,0:T(8,128)(2,1)S(1)}, u32[]{:S(2)}, u32[]{:S(2)}) %all-to-all-start.1) | async-done | bytes 1048608 | tf_op jit(solution)/shard_map/sums_to_all/all_to_all | solution.py:360
  92.7 0.9 collective-permute-start.1
  93.6 1.4 %fill_own.1 = (f32[1024,512]{1,0:T(8,128)}, f32[512,512]{1,0:T(8,128)}, f32[512,512]{1,0:T(8,128)}) custom-call(s32[1]{0:T(128)} %bitcast.me, bf16[64,2,32,128]{3,2,1,0:T(8,128)(2,1)S(1)} %bitcast.14), custom_call_target="tpu_custom_call" | custom-call | flops 524288 | bytes 3145728 | tf_op jit(solution)/shard_map/fill_own/pallas_call | solution.py:396
  95.0 0.9 collective-permute-done.1
  95.9 1.4 %fill_other.1 = (f32[1024,512]{1,0:T(8,128)}, f32[512,512]{1,0:T(8,128)}, f32[512,512]{1,0:T(8,128)}) custom-call(s32[1]{0:T(128)} %bitcast.me, bf16[64,2,32,128]{3,2,1,0:T(8,128)(2,1)S(1)} %bitcast.15, f32[1024,512]{1,0:T(8,128)} %get-tuple-element.35.refs_0_, ...), custom_call_target="tpu_custom_call", output_to_operand_aliasing={{0}: (2, {}), {1}: (3, {}), {2}: (4, {})} | custom-call | flops 524288 | bytes 3145728 | tf_op jit(solution)/shard_map/fill_other/pallas_call | solution.py:396
Async XLA Ops:
  4.9 4.0 %collective-permute-start = (bf16[1024,512]{1,0:T(8,128)(2,1)S(1)}, bf16[1024,512]{1,0:T(8,128)(2,1)S(1)}, u32[]{:S(2)}, u32[]{:S(2)}) collective-permute-start(bf16[1024,512]{1,0:T(8,128)(2,1)S(1)} %get-tuple-element.24), channel_id=1, source_target_pairs={{0,1},{1,0},{2,3},{3,2},{4,5},{5,4},{6,7},{7,6},{8,9},{9,8},{10,11... | collective-permute-start | bytes 3145736 | tf_op jit(solution)/shard_map/core_exchange/ppermute | solution.py:321
  68.8 23.9 %all-to-all-start.1 = ((bf16[128,32,128]{2,1,0:T(8,128)(2,1)}), bf16[128,32,128]{2,1,0:T(8,128)(2,1)S(1)}, u32[]{:S(2)}, u32[]{:S(2)}) async-start(bf16[128,32,128]{2,1,0:T(8,128)(2,1)} %bitcast.16), calls=%async_computation.1 | async-start | bytes 2097152 | tf_op jit(solution)/shard_map/sums_to_all/all_to_all | solution.py:360
  92.7 3.2 %collective-permute-start.1 = (bf16[128,32,128]{2,1,0:T(8,128)(2,1)S(1)}, bf16[128,32,128]{2,1,0:T(8,128)(2,1)S(1)}, u32[]{:S(2)}, u32[]{:S(2)}) collective-permute-start(bf16[128,32,128]{2,1,0:T(8,128)(2,1)S(1)} %all-to-all-done.1), channel_id=1, source_target_pairs={{0,1},{1,0},{2,3},{3,2},{4,5},{5,4},{6,7},{7,6},{8,9},{9,8},{10,11... | collective-permute-start | bytes 3145736 | tf_op jit(solution)/shard_map/core_exchange_back/ppermute | solution.py:391

commit v5 on v4

--- a/solution.py
+++ b/solution.py
@@ -59,80 +59,29 @@
     return mm(by_rank, onehot((rank < CAP) & (target == kind * 128 + lane)))
 
 
-def grads_kernel(
-    me, h_in, a_in, go_in, ws_in, wn_in, hub_in, owner_in, slot_in,
-    g_out, message, mine, send, owner, slot,
-    h, a, go, ws, wn, hub, g, arrived,
-):
-    loads = [
-        pltpu.make_async_copy(src, dst, arrived.at[i])
-        for i, (src, dst) in enumerate(
-            (
-                (h_in, h), (ws_in, ws), (a_in, a), (wn_in, wn), (go_in, go), (hub_in, hub),
-                (owner_in, owner), (slot_in, slot),
-            )
-        )
-    ]
-    for load in loads:
-        load.start()
-
-    t = h.shape[0]
-    loads[0].wait()
-    loads[1].wait()
-    pre = mm(h[...], ws[...])
-    loads[2].wait()
-    loads[3].wait()
-    pre = pre + mm(a[...], wn[...])
-    loads[4].wait()
-    sig = jax.nn.sigmoid(pre)
-    g[...] = (go[...].astype(F32) * (sig * (1.0 + pre * (1.0 - sig)))).astype(BF)
-    store = pltpu.make_async_copy(g, g_out, arrived.at[8])
-    store.start()
-    msg = (mm_nt(g[...], wn[...]) / FANOUT).astype(BF)
-    message[...] = msg
-    loads[5].wait()
-    rows = lax.broadcasted_iota(I16, (HUBS, t), 0)
+def hub_sums(message, hub):
+    rows = lax.broadcasted_iota(I16, (HUBS, message.shape[0]), 0)
     ids = hub[...].astype(I16)
     count = onehot(rows == ids[0:1, :]) + onehot(rows == ids[1:2, :])
-    hub_part = mm(count, msg).astype(BF)
+    return mm(count, message[...]).astype(BF)
+
+
+def half_sums(hubs, message, hub, h, a, g, out):
     depth = h.shape[1]
-    first = lax.rem(me[0], 2) == 0
-    part_self = mm_tn(h[...], g[...]).astype(BF)
-    part_neigh = mm_tn(a[...], g[...]).astype(BF)
-
-    @pl.when(first)
+
+    @pl.when(hubs)
     def _():
-        mine[...] = hub_part
-        send[0:depth, :] = part_self
-        send[depth : 2 * depth, :] = part_neigh
-
-    @pl.when(jnp.logical_not(first))
+        out[...] = hub_sums(message, hub)
+
+    @pl.when(jnp.logical_not(hubs))
     def _():
-        send[...] = hub_part
-        mine[0:depth, :] = part_self
-        mine[depth : 2 * depth, :] = part_neigh
-
-    store.wait()
-    loads[6].wait()
-    loads[7].wait()
-
-
-def spread_rows():
-    row = lax.broadcasted_iota(I32, (GROUP * 16, 192), 0)
-    col = lax.broadcasted_iota(I32, (GROUP * 16, 192), 1)
-    chunk, s = row // 16, row % 16
-    want = jnp.where(s < 8, (s // 2) * 32 + chunk * 2 + s % 2, 128 + (s - 8) * 16 + chunk)
-    return onehot((s < 12) & (col == want))
-
-
-def picks(places, at):
-    return onehot((at == places[0]) | (at == places[1]) | (at == places[2]))
-
-
-def pack_kernel(me, owner, slot, message, out):
-    t = message.shape[0]
-    n = out.shape[0]
-    fan = slot.shape[0]
+        out[0:depth, :] = mm_tn(h[...], g[...]).astype(BF)
+        out[depth : 2 * depth, :] = mm_tn(a[...], g[...]).astype(BF)
+
+
+def find_places(chip_row, owner, slot, places, kinds):
+    fan, t = slot.shape
+    n = kinds.shape[0]
     device = lax.broadcasted_iota(I32, (n, t), 0)
     before = onehot(
         lax.broadcasted_iota(I16, (t, t), 0) < lax.broadcasted_iota(I16, (t, t), 1)
@@ -148,13 +97,68 @@
         rank = jnp.where(named[j], earlier[j * n : (j + 1) * n, :] + base, 0.0)
         ranks.append(jnp.sum(rank, axis=0, keepdims=True).astype(I32))
         base = base + amount[j * n : (j + 1) * n, :]
-    main, last = [], []
     for j, rank in enumerate(ranks):
         in_main = rank < MAIN
-        main.append(jnp.where(in_main, owner[j] * MAIN + rank, -1).astype(I16))
-        last.append(jnp.where(in_main, -1, owner[j] * REST + (rank - MAIN)).astype(I16))
-    kinds = slot_kinds(me[0], slot[...], hots, ranks).astype(BF)
-
+        places[j : j + 1, :] = jnp.where(in_main, owner[j] * MAIN + rank, -1)
+        places[4 + j : 5 + j, :] = jnp.where(in_main, -1, owner[j] * REST + (rank - MAIN))
+    kinds[...] = slot_kinds(chip_row, slot[...], hots, ranks).astype(BF)
+
+
+def grads_kernel(
+    me, h_in, a_in, go_in, ws_in, wn_in, hub_in, owner_in, slot_in,
+    g_out, h, a, g, hub, message, send, places, kinds,
+    go, ws, wn, owner, slot, arrived,
+):
+    loads = [
+        pltpu.make_async_copy(src, dst, arrived.at[i])
+        for i, (src, dst) in enumerate(
+            (
+                (owner_in, owner), (slot_in, slot),
+                (h_in, h), (ws_in, ws), (a_in, a), (wn_in, wn), (go_in, go), (hub_in, hub),
+            )
+        )
+    ]
+    for load in loads:
+        load.start()
+
+    loads[0].wait()
+    loads[1].wait()
+    find_places(me[0], owner, slot, places, kinds)
+    loads[2].wait()
+    loads[3].wait()
+    pre = mm(h[...], ws[...])
+    loads[4].wait()
+    loads[5].wait()
+    pre = pre + mm(a[...], wn[...])
+    loads[6].wait()
+    sig = jax.nn.sigmoid(pre)
+    g[...] = (go[...].astype(F32) * (sig * (1.0 + pre * (1.0 - sig)))).astype(BF)
+    store = pltpu.make_async_copy(g, g_out, arrived.at[8])
+    store.start()
+    message[...] = (mm_nt(g[...], wn[...]) / FANOUT).astype(BF)
+    loads[7].wait()
+    half_sums(lax.rem(me[0], 2) == 1, message, hub, h, a, g, send)
+    store.wait()
+
+
+def spread_rows():
+    row = lax.broadcasted_iota(I32, (GROUP * 16, 192), 0)
+    col = lax.broadcasted_iota(I32, (GROUP * 16, 192), 1)
+    chunk, s = row // 16, row % 16
+    want = jnp.where(s < 8, (s // 2) * 32 + chunk * 2 + s % 2, 128 + (s - 8) * 16 + chunk)
+    return onehot((s < 12) & (col == want))
+
+
+def picks(places, at):
+    return onehot((at == places[0]) | (at == places[1]) | (at == places[2]))
+
+
+def pack_kernel(me, h, a, g, hub, message, places, kinds, out, mine):
+    t = message.shape[0]
+    n = out.shape[0]
+    half_sums(lax.rem(me[0], 2) == 0, message, hub, h, a, g, mine)
+    main = [places[j : j + 1, :].astype(I16) for j in range(3)]
+    last = [places[4 + j : 5 + j, :].astype(I16) for j in range(3)]
     msg = message[...]
     spread = spread_rows()
     rest = mm(picks(last, lax.broadcasted_iota(I16, (n * REST, t), 0)), msg).astype(BF)
@@ -296,23 +300,27 @@
     swap = [(i, i ^ 1) for i in range(n)]
 
     with jax.named_scope("grads"):
-        g, message, mine, send, owner_v, slot_v = pl.pallas_call(
+        g_kept, h, a, g, hub, message, send, places, kinds = pl.pallas_call(
             grads_kernel,
             out_shape=(
                 pltpu.HBM((t, width), BF),
                 pltpu.VMEM((t, width), BF),
+                pltpu.VMEM((t, width), BF),
+                pltpu.VMEM((t, width), BF),
+                pltpu.VMEM(hub_t.shape, I32),
+                pltpu.VMEM((t, width), BF),
                 pltpu.VMEM((HUBS, width), BF),
-                pltpu.VMEM((HUBS, width), BF),
+                pltpu.VMEM((8, t), I32),
+                pltpu.VMEM((n, 512), BF),
+            ),
+            in_specs=[SMEM] + [HBM] * 8,
+            out_specs=[HBM] + [VMEM] * 8,
+            scratch_shapes=[
+                pltpu.VMEM((t, width), BF),
+                pltpu.VMEM((width, width), BF),
+                pltpu.VMEM((width, width), BF),
                 pltpu.VMEM(owner_t.shape, I32),
                 pltpu.VMEM(slot_t.shape, I32),
-            ),
-            in_specs=[SMEM] + [HBM] * 8,
-            out_specs=[HBM] + [VMEM] * 5,
-            scratch_shapes=[pltpu.VMEM((t, width), BF)] * 3
-            + [pltpu.VMEM((width, width), BF)] * 2
-            + [
-                pltpu.VMEM(hub_t.shape, I32),
-                pltpu.VMEM((t, width), BF),
                 pltpu.SemaphoreType.DMA((9,)),
             ],
             compiler_params=PARAMS,
@@ -320,13 +328,13 @@
     with jax.named_scope("core_exchange"):
         got = lax.ppermute(send, "dev", swap)
     with jax.named_scope("pack"):
-        packed = pl.pallas_call(
+        packed, mine = pl.pallas_call(
             pack_kernel,
-            out_shape=pltpu.VMEM((n, CHUNK, 128), BF),
-            in_specs=[SMEM] + [VMEM] * 3,
-            out_specs=VMEM,
+            out_shape=(pltpu.VMEM((n, CHUNK, 128), BF), pltpu.VMEM((HUBS, width), BF)),
+            in_specs=[SMEM] + [VMEM] * 7,
+            out_specs=[VMEM] * 2,
             compiler_params=PARAMS,
-        )(me, *map(in_vmem, (owner_v, slot_v, message)))
+        )(me, *map(in_vmem, (h, a, g, hub, message, places, kinds)))
     with jax.named_scope("join"):
         packed = pl.pallas_call(
             join_kernel,
@@ -385,7 +393,7 @@
             cost_estimate=pl.CostEstimate(
                 flops=2 * OWN_DEV * n * CAP * width, bytes_accessed=8 << 20, transcendentals=0
             ),
-        )(in_hbm(kept), in_hbm(g), in_hbm(w_self))
+        )(in_hbm(kept), in_hbm(g_kept), in_hbm(w_self))
     own, front_grad = lax.optimization_barrier((own, front_grad))
     with jax.named_scope("core_exchange_back"):
         other = lax.ppermute(own, "dev", swap)

time: 97.5 us -> 96.9 us (level)
  no operation moved by 1% of the time
where the time goes in v5:
time: 96.9 us; the launch traced here: 96.7 us
  blocking collectives  57.5 us (59%)
  Pallas kernels  23.4 us (24%)
  waiting for transfers between devices  8.18 us (8%)
  starting transfers between devices  7 us (7%)
    all_to_all x1, blocking collectives, body(): lax.all_to_all(packed.reshape(n, CHUNK, 128), 'dev', split_axis=0, concat...  57.5 us
    pallas_call x1, Pallas kernels, body(): pl.pallas_call(front_kernel, out_shape=(jax.ShapeDtypeStruct((OWN_DEV, wi...  12 us
    all_to_all x1, waiting for transfers between devices, body(): lax.all_to_all(total.reshape(n, 32, 128), 'dev', split_axis=0, concat_axi...  7.3 us
    all_to_all x1, starting transfers between devices, body(): lax.all_to_all(total.reshape(n, 32, 128), 'dev', split_axis=0, concat_axi...  4.6 us
    pallas_call x1, Pallas kernels, body(): pl.pallas_call(grads_kernel, out_shape=(pltpu.HBM((t, width), BF), pltpu....  3.65 us
    pallas_call x2, Pallas kernels, body(): pl.pallas_call(functools.partial(fill_kernel, scale, mine_too), out_shape...  2.82 us
    pallas_call x1, Pallas kernels, body(): pl.pallas_call(pack_kernel, out_shape=(pltpu.VMEM((n, CHUNK, 128), BF), p...  2.51 us
    pallas_call x1, Pallas kernels, body(): pl.pallas_call(reduce_kernel, out_shape=(pltpu.HBM((n // 2, 2, 32, 128),...  2.09 us
  transfers between devices with their start and end apart: 3, of which 2 were waited for; matrix products, arithmetic and copies ran while one was open for 0% of the time, Pallas kernels for 16%

profile of v5, /device:TPU:1, one launch (start us, length us, event | category | flops | bytes accessed | tf_op | source)
XLA Modules:
  0.0 96.7 jit_solution(2237585755191604043)
XLA Ops:
  0.6 3.6 %grads.1 = (bf16[512,512]{1,0:T(8,128)(2,1)}, bf16[512,512]{1,0:T(8,128)(2,1)S(1)}, bf16[512,512]{1,0:T(8,128)(2,1)S(1)}, bf16[512,512]{1,0:T(8,128)(2,1)S(1)}, ...) custom-call(s32[1]{0:T(128)} %bitcast.me, ...), custom_call_target="tpu_custom_call" | custom-call | tf_op jit(solution)/shard_map/grads/pallas_call | solution.py:303
  4.3 1.5 %collective-permute-start = (bf16[1024,512]{1,0:T(8,128)(2,1)S(1)}, bf16[1024,512]{1,0:T(8,128)(2,1)S(1)}, u32[]{:S(2)}, u32[]{:S(2)}) collective-permute-start(bf16[1024,512]{1,0:T(8,128)(2,1)S(1)} %get-tuple-element.36), channel_id=1, source_target_pairs={{0,1},{1,0},{2,3},{3,2},{4,5},{5,4},{6,7},{7,6},{8,9},{9,8},{10,11... | collective-permute-start | bytes 3145736 | tf_op jit(solution)/shard_map/core_exchange/ppermute | solution.py:329
  5.8 2.5 %pack.1 = (bf16[128,112,128]{2,1,0:T(8,128)(2,1)S(1)}, bf16[1024,512]{1,0:T(8,128)(2,1)S(1)}) custom-call(s32[1]{0:T(128)} %bitcast.me, bf16[512,512]{1,0:T(8,128)(2,1)S(1)} %get-tuple-element.28.h, bf16[512,512]{1,0:T(8,128)(2,1)S(1)} %get-tuple-element.29.a, bf16[512,512]{1,0:T(8,128)(2,1)S(1)} %get-tuple-element.30.g, ...), custom_call_target="tpu_custom_call" | custom-call | tf_op jit(solution)/shard_map/pack/pallas_call | solution.py:331
  8.3 0.0 collective-permute-done.got
  8.3 0.3 join.1
  8.6 57.5 %all_to_all.10 = bf16[128,112,128]{2,1,0:T(8,128)(2,1)S(1)} all-to-all(bf16[128,112,128]{2,1,0:T(8,128)(2,1)S(1)} %bitcast.12), channel_id=1, replica_groups=mesh['dev'=128] {'dev'}, dimensions={0} | all-to-all | bytes 7340032 | tf_op jit(solution)/shard_map/rows_to_owners/all_to_all | solution.py:348
  66.1 2.1 %sum_parts.1 = (bf16[64,2,32,128]{3,2,1,0:T(8,128)(2,1)}, bf16[64,2,80,128]{3,2,1,0:T(8,128)(2,1)}) custom-call(bf16[64,2,112,128]{3,2,1,0:T(8,128)(2,1)S(1)} %bitcast.13), custom_call_target="tpu_custom_call" | custom-call | tf_op jit(solution)/shard_map/sum_parts/pallas_call | solution.py:352
  68.2 4.6 %all-to-all-start.1 = ((bf16[128,32,128]{2,1,0:T(8,128)(2,1)}), bf16[128,32,128]{2,1,0:T(8,128)(2,1)S(1)}, u32[]{:S(2)}, u32[]{:S(2)}) async-start(bf16[128,32,128]{2,1,0:T(8,128)(2,1)} %bitcast.16), calls=%async_computation.1 | async-start | bytes 2097152 | tf_op jit(solution)/shard_map/sums_to_all/all_to_all | solution.py:368
  72.8 12.0 %front.1 = (f32[2048,512]{1,0:T(8,128)}, bf16[512,512]{1,0:T(8,128)(2,1)}) custom-call(bf16[128,80,128]{2,1,0:T(8,128)(2,1)} %bitcast.20, bf16[512,512]{1,0:T(8,128)(2,1)} %get-tuple-element.39.g, bf16[512,512]{1,0:T(8,128)(2,1)} %ws.1), custom_call_target="tpu_custom_call" | custom-call | flops 4831838208 | bytes 8388608 | tf_op jit(solution)/shard_map/front/pallas_call | solution.py:372
  84.8 7.3 %all-to-all-done.1 = bf16[128,32,128]{2,1,0:T(8,128)(2,1)S(1)} async-done(((bf16[128,32,128]{2,1,0:T(8,128)(2,1)}), bf16[128,32,128]{2,1,0:T(8,128)(2,1)S(1)}, u32[]{:S(2)}, u32[]{:S(2)}) %all-to-all-start.1) | async-done | bytes 1048608 | tf_op jit(solution)/shard_map/sums_to_all/all_to_all | solution.py:368
  92.1 0.9 collective-permute-start.1
  93.0 1.4 %fill_own.1 = (f32[1024,512]{1,0:T(8,128)}, f32[512,512]{1,0:T(8,128)}, f32[512,512]{1,0:T(8,128)}) custom-call(s32[1]{0:T(128)} %bitcast.me, bf16[64,2,32,128]{3,2,1,0:T(8,128)(2,1)S(1)} %bitcast.14), custom_call_target="tpu_custom_call" | custom-call | flops 524288 | bytes 3145728 | tf_op jit(solution)/shard_map/fill_own/pallas_call | solution.py:404
  94.4 0.9 collective-permute-done.1
  95.3 1.4 %fill_other.1 = (f32[1024,512]{1,0:T(8,128)}, f32[512,512]{1,0:T(8,128)}, f32[512,512]{1,0:T(8,128)}) custom-call(s32[1]{0:T(128)} %bitcast.me, bf16[64,2,32,128]{3,2,1,0:T(8,128)(2,1)S(1)} %bitcast.15, f32[1024,512]{1,0:T(8,128)} %get-tuple-element.45.refs_0_, ...), custom_call_target="tpu_custom_call", output_to_operand_aliasing={{0}: (2, {}), {1}: (3, {}), {2}: (4, {})} | custom-call | flops 524288 | bytes 3145728 | tf_op jit(solution)/shard_map/fill_other/pallas_call | solution.py:404
Async XLA Ops:
  4.3 4.0 %collective-permute-start = (bf16[1024,512]{1,0:T(8,128)(2,1)S(1)}, bf16[1024,512]{1,0:T(8,128)(2,1)S(1)}, u32[]{:S(2)}, u32[]{:S(2)}) collective-permute-start(bf16[1024,512]{1,0:T(8,128)(2,1)S(1)} %get-tuple-element.36), channel_id=1, source_target_pairs={{0,1},{1,0},{2,3},{3,2},{4,5},{5,4},{6,7},{7,6},{8,9},{9,8},{10,11... | collective-permute-start | bytes 3145736 | tf_op jit(solution)/shard_map/core_exchange/ppermute | solution.py:329
  68.2 23.9 %all-to-all-start.1 = ((bf16[128,32,128]{2,1,0:T(8,128)(2,1)}), bf16[128,32,128]{2,1,0:T(8,128)(2,1)S(1)}, u32[]{:S(2)}, u32[]{:S(2)}) async-start(bf16[128,32,128]{2,1,0:T(8,128)(2,1)} %bitcast.16), calls=%async_computation.1 | async-start | bytes 2097152 | tf_op jit(solution)/shard_map/sums_to_all/all_to_all | solution.py:368
  92.1 3.2 %collective-permute-start.1 = (bf16[128,32,128]{2,1,0:T(8,128)(2,1)S(1)}, bf16[128,32,128]{2,1,0:T(8,128)(2,1)S(1)}, u32[]{:S(2)}, u32[]{:S(2)}) collective-permute-start(bf16[128,32,128]{2,1,0:T(8,128)(2,1)S(1)} %all-to-all-done.1), channel_id=1, source_target_pairs={{0,1},{1,0},{2,3},{3,2},{4,5},{5,4},{6,7},{7,6},{8,9},{9,8},{10,11... | collective-permute-start | bytes 3145736 | tf_op jit(solution)/shard_map/core_exchange_back/ppermute | solution.py:399

commit v6 on v5

--- a/solution.py
+++ b/solution.py
@@ -187,19 +187,19 @@
 
 def reduce_kernel(received, out, kept, total, left):
     chips, each = received.shape[0], total.shape[0]
+    rows = pltpu.make_async_copy(received.at[:, :, pl.ds(0, FRONT), :], kept, left.at[0])
+    rows.start()
     acc = jnp.sum(received[:, :, FRONT : FRONT + 32, :].astype(F32), axis=0, keepdims=True)
     total[...] = jnp.broadcast_to(acc.astype(BF), total.shape)
     copies = [
         pltpu.make_async_copy(total, out.at[pl.ds(i * each, each)], left.at[1 + i])
         for i in range(chips // each)
     ]
-    copies.append(
-        pltpu.make_async_copy(received.at[:, :, pl.ds(0, FRONT), :], kept, left.at[0])
-    )
     for copy in copies:
         copy.start()
     for copy in copies:
         copy.wait()
+    rows.wait()
 
 
 def front_kernel(received, g, ws, out, grad_self, rows, index):

time: 96.9 us -> 96.7 us (level)
  transfers between devices with their start and end apart: 3 -> 3, of which waited for: 2 -> 2; matrix products, arithmetic and copies ran while one was open for 0% -> 0% of each run, Pallas kernels for 16% -> 17%
where the time goes in v6:
time: 96.7 us; the launch traced here: 96.5 us
  blocking collectives  57.5 us (59%)
  Pallas kernels  23.2 us (24%)
  waiting for transfers between devices  8.17 us (8%)
  starting transfers between devices  7 us (7%)
    all_to_all x1, blocking collectives, body(): lax.all_to_all(packed.reshape(n, CHUNK, 128), 'dev', split_axis=0, concat...  57.5 us
    pallas_call x1, Pallas kernels, body(): pl.pallas_call(front_kernel, out_shape=(jax.ShapeDtypeStruct((OWN_DEV, wi...  12 us
    all_to_all x1, waiting for transfers between devices, body(): lax.all_to_all(total.reshape(n, 32, 128), 'dev', split_axis=0, concat_axi...  7.3 us
    all_to_all x1, starting transfers between devices, body(): lax.all_to_all(total.reshape(n, 32, 128), 'dev', split_axis=0, concat_axi...  4.6 us
    pallas_call x1, Pallas kernels, body(): pl.pallas_call(grads_kernel, out_shape=(pltpu.HBM((t, width), BF), pltpu....  3.65 us
    pallas_call x2, Pallas kernels, body(): pl.pallas_call(functools.partial(fill_kernel, scale, mine_too), out_shape...  2.82 us
    pallas_call x1, Pallas kernels, body(): pl.pallas_call(pack_kernel, out_shape=(pltpu.VMEM((n, CHUNK, 128), BF), p...  2.51 us
  transfers between devices with their start and end apart: 3, of which 2 were waited for; matrix products, arithmetic and copies ran while one was open for 0% of the time, Pallas kernels for 17%

profile of v6, /device:TPU:1, one launch (start us, length us, event | category | flops | bytes accessed | tf_op | source)
XLA Modules:
  0.0 96.5 jit_solution(12027471967292141556)
XLA Ops:
  0.6 3.6 %grads.1 = (bf16[512,512]{1,0:T(8,128)(2,1)}, bf16[512,512]{1,0:T(8,128)(2,1)S(1)}, bf16[512,512]{1,0:T(8,128)(2,1)S(1)}, bf16[512,512]{1,0:T(8,128)(2,1)S(1)}, ...) custom-call(s32[1]{0:T(128)} %bitcast.me, ...), custom_call_target="tpu_custom_call" | custom-call | tf_op jit(solution)/shard_map/grads/pallas_call | solution.py:303
  4.3 1.5 %collective-permute-start = (bf16[1024,512]{1,0:T(8,128)(2,1)S(1)}, bf16[1024,512]{1,0:T(8,128)(2,1)S(1)}, u32[]{:S(2)}, u32[]{:S(2)}) collective-permute-start(bf16[1024,512]{1,0:T(8,128)(2,1)S(1)} %get-tuple-element.36), channel_id=1, source_target_pairs={{0,1},{1,0},{2,3},{3,2},{4,5},{5,4},{6,7},{7,6},{8,9},{9,8},{10,11... | collective-permute-start | bytes 3145736 | tf_op jit(solution)/shard_map/core_exchange/ppermute | solution.py:329
  5.8 2.5 %pack.1 = (bf16[128,112,128]{2,1,0:T(8,128)(2,1)S(1)}, bf16[1024,512]{1,0:T(8,128)(2,1)S(1)}) custom-call(s32[1]{0:T(128)} %bitcast.me, bf16[512,512]{1,0:T(8,128)(2,1)S(1)} %get-tuple-element.28.h, bf16[512,512]{1,0:T(8,128)(2,1)S(1)} %get-tuple-element.29.a, bf16[512,512]{1,0:T(8,128)(2,1)S(1)} %get-tuple-element.30.g, ...), custom_call_target="tpu_custom_call" | custom-call | tf_op jit(solution)/shard_map/pack/pallas_call | solution.py:331
  8.3 0.0 collective-permute-done.got
  8.3 0.3 join.1
  8.6 57.5 %all_to_all.10 = bf16[128,112,128]{2,1,0:T(8,128)(2,1)S(1)} all-to-all(bf16[128,112,128]{2,1,0:T(8,128)(2,1)S(1)} %bitcast.12), channel_id=1, replica_groups=mesh['dev'=128] {'dev'}, dimensions={0} | all-to-all | bytes 7340032 | tf_op jit(solution)/shard_map/rows_to_owners/all_to_all | solution.py:348
  66.1 1.9 %sum_parts.1 = (bf16[64,2,32,128]{3,2,1,0:T(8,128)(2,1)}, bf16[64,2,80,128]{3,2,1,0:T(8,128)(2,1)}) custom-call(bf16[64,2,112,128]{3,2,1,0:T(8,128)(2,1)S(1)} %bitcast.13), custom_call_target="tpu_custom_call" | custom-call | tf_op jit(solution)/shard_map/sum_parts/pallas_call | solution.py:352
  68.0 4.6 %all-to-all-start.1 = ((bf16[128,32,128]{2,1,0:T(8,128)(2,1)}), bf16[128,32,128]{2,1,0:T(8,128)(2,1)S(1)}, u32[]{:S(2)}, u32[]{:S(2)}) async-start(bf16[128,32,128]{2,1,0:T(8,128)(2,1)} %bitcast.16), calls=%async_computation.1 | async-start | bytes 2097152 | tf_op jit(solution)/shard_map/sums_to_all/all_to_all | solution.py:368
  72.6 12.0 %front.1 = (f32[2048,512]{1,0:T(8,128)}, bf16[512,512]{1,0:T(8,128)(2,1)}) custom-call(bf16[128,80,128]{2,1,0:T(8,128)(2,1)} %bitcast.20, bf16[512,512]{1,0:T(8,128)(2,1)} %get-tuple-element.39.g, bf16[512,512]{1,0:T(8,128)(2,1)} %ws.1), custom_call_target="tpu_custom_call" | custom-call | flops 4831838208 | bytes 8388608 | tf_op jit(solution)/shard_map/front/pallas_call | solution.py:372
  84.6 7.3 %all-to-all-done.1 = bf16[128,32,128]{2,1,0:T(8,128)(2,1)S(1)} async-done(((bf16[128,32,128]{2,1,0:T(8,128)(2,1)}), bf16[128,32,128]{2,1,0:T(8,128)(2,1)S(1)}, u32[]{:S(2)}, u32[]{:S(2)}) %all-to-all-start.1) | async-done | bytes 1048608 | tf_op jit(solution)/shard_map/sums_to_all/all_to_all | solution.py:368
  91.9 0.9 collective-permute-start.1
  92.8 1.4 %fill_own.1 = (f32[1024,512]{1,0:T(8,128)}, f32[512,512]{1,0:T(8,128)}, f32[512,512]{1,0:T(8,128)}) custom-call(s32[1]{0:T(128)} %bitcast.me, bf16[64,2,32,128]{3,2,1,0:T(8,128)(2,1)S(1)} %bitcast.14), custom_call_target="tpu_custom_call" | custom-call | flops 524288 | bytes 3145728 | tf_op jit(solution)/shard_map/fill_own/pallas_call | solution.py:404
  94.2 0.9 collective-permute-done.1
  95.1 1.4 %fill_other.1 = (f32[1024,512]{1,0:T(8,128)}, f32[512,512]{1,0:T(8,128)}, f32[512,512]{1,0:T(8,128)}) custom-call(s32[1]{0:T(128)} %bitcast.me, bf16[64,2,32,128]{3,2,1,0:T(8,128)(2,1)S(1)} %bitcast.15, f32[1024,512]{1,0:T(8,128)} %get-tuple-element.45.refs_0_, ...), custom_call_target="tpu_custom_call", output_to_operand_aliasing={{0}: (2, {}), {1}: (3, {}), {2}: (4, {})} | custom-call | flops 524288 | bytes 3145728 | tf_op jit(solution)/shard_map/fill_other/pallas_call | solution.py:404
Async XLA Ops:
  4.3 4.0 %collective-permute-start = (bf16[1024,512]{1,0:T(8,128)(2,1)S(1)}, bf16[1024,512]{1,0:T(8,128)(2,1)S(1)}, u32[]{:S(2)}, u32[]{:S(2)}) collective-permute-start(bf16[1024,512]{1,0:T(8,128)(2,1)S(1)} %get-tuple-element.36), channel_id=1, source_target_pairs={{0,1},{1,0},{2,3},{3,2},{4,5},{5,4},{6,7},{7,6},{8,9},{9,8},{10,11... | collective-permute-start | bytes 3145736 | tf_op jit(solution)/shard_map/core_exchange/ppermute | solution.py:329
  68.0 23.9 %all-to-all-start.1 = ((bf16[128,32,128]{2,1,0:T(8,128)(2,1)}), bf16[128,32,128]{2,1,0:T(8,128)(2,1)S(1)}, u32[]{:S(2)}, u32[]{:S(2)}) async-start(bf16[128,32,128]{2,1,0:T(8,128)(2,1)} %bitcast.16), calls=%async_computation.1 | async-start | bytes 2097152 | tf_op jit(solution)/shard_map/sums_to_all/all_to_all | solution.py:368
  91.9 3.2 %collective-permute-start.1 = (bf16[128,32,128]{2,1,0:T(8,128)(2,1)S(1)}, bf16[128,32,128]{2,1,0:T(8,128)(2,1)S(1)}, u32[]{:S(2)}, u32[]{:S(2)}) collective-permute-start(bf16[128,32,128]{2,1,0:T(8,128)(2,1)S(1)} %all-to-all-done.1), channel_id=1, source_target_pairs={{0,1},{1,0},{2,3},{3,2},{4,5},{5,4},{6,7},{7,6},{8,9},{9,8},{10,11... | collective-permute-start | bytes 3145736 | tf_op jit(solution)/shard_map/core_exchange_back/ppermute | solution.py:399

commit v7 on v6

--- a/solution.py
+++ b/solution.py
@@ -162,14 +162,21 @@
     msg = message[...]
     spread = spread_rows()
     rest = mm(picks(last, lax.broadcasted_iota(I16, (n * REST, t), 0)), msg).astype(BF)
-    for g in range(n // GROUP):
-        stacked = jnp.concatenate(
-            [rest[g * 32 : (g + 1) * 32, q * 128 : (q + 1) * 128] for q in range(4)]
-            + [kinds[g * GROUP : (g + 1) * GROUP, q * 128 : (q + 1) * 128] for q in range(4)],
-            axis=0,
-        )
-        out[g * GROUP : (g + 1) * GROUP, 64:80, :] = (
-            mm(spread, stacked).astype(BF).reshape(GROUP, 16, 128)
+    stacked = jnp.concatenate(
+        [
+            jnp.concatenate(
+                [rest[k * 32 : (k + 1) * 32, q * 128 : (q + 1) * 128] for q in range(4)]
+                + [kinds[k * GROUP : (k + 1) * GROUP, q * 128 : (q + 1) * 128] for q in range(4)],
+                axis=0,
+            )
+            for k in range(n // GROUP)
+        ],
+        axis=1,
+    )
+    tiles = mm(spread, stacked).astype(BF)
+    for k in range(n // GROUP):
+        out[k * GROUP : (k + 1) * GROUP, 64:80, :] = tiles[:, k * 128 : (k + 1) * 128].reshape(
+            GROUP, 16, 128
         )
     rows = mm(picks(main, lax.broadcasted_iota(I16, (n * MAIN, t), 0)), msg).astype(BF)
     for q in range(4):

time: 96.7 us -> 96.7 us (level)
  transfers between devices with their start and end apart: 3 -> 3, of which waited for: 2 -> 2; matrix products, arithmetic and copies ran while one was open for 0% -> 0% of each run, Pallas kernels for 17% -> 16%
where the time goes in v7:
time: 96.7 us; the launch traced here: 96.5 us
  blocking collectives  57.6 us (60%)
  Pallas kernels  23 us (24%)
  waiting for transfers between devices  8.18 us (8%)
  starting transfers between devices  7 us (7%)
    all_to_all x1, blocking collectives, body(): lax.all_to_all(packed.reshape(n, CHUNK, 128), 'dev', split_axis=0, concat...  57.6 us
    pallas_call x1, Pallas kernels, body(): pl.pallas_call(front_kernel, out_shape=(jax.ShapeDtypeStruct((OWN_DEV, wi...  12 us
    all_to_all x1, waiting for transfers between devices, body(): lax.all_to_all(total.reshape(n, 32, 128), 'dev', split_axis=0, concat_axi...  7.31 us
    all_to_all x1, starting transfers between devices, body(): lax.all_to_all(total.reshape(n, 32, 128), 'dev', split_axis=0, concat_axi...  4.6 us
    pallas_call x1, Pallas kernels, body(): pl.pallas_call(grads_kernel, out_shape=(pltpu.HBM((t, width), BF), pltpu....  3.65 us
    pallas_call x2, Pallas kernels, body(): pl.pallas_call(functools.partial(fill_kernel, scale, mine_too), out_shape...  2.82 us
    pallas_call x1, Pallas kernels, body(): pl.pallas_call(pack_kernel, out_shape=(pltpu.VMEM((n, CHUNK, 128), BF), p...  2.38 us
  transfers between devices with their start and end apart: 3, of which 2 were waited for; matrix products, arithmetic and copies ran while one was open for 0% of the time, Pallas kernels for 16%

profile of v7, /device:TPU:1, one launch (start us, length us, event | category | flops | bytes accessed | tf_op | source)
XLA Modules:
  0.0 96.5 jit_solution(4757123574519052185)
XLA Ops:
  0.6 3.6 %grads.1 = (bf16[512,512]{1,0:T(8,128)(2,1)}, bf16[512,512]{1,0:T(8,128)(2,1)S(1)}, bf16[512,512]{1,0:T(8,128)(2,1)S(1)}, bf16[512,512]{1,0:T(8,128)(2,1)S(1)}, ...) custom-call(s32[1]{0:T(128)} %bitcast.me, ...), custom_call_target="tpu_custom_call" | custom-call | tf_op jit(solution)/shard_map/grads/pallas_call | solution.py:310
  4.3 1.5 %collective-permute-start = (bf16[1024,512]{1,0:T(8,128)(2,1)S(1)}, bf16[1024,512]{1,0:T(8,128)(2,1)S(1)}, u32[]{:S(2)}, u32[]{:S(2)}) collective-permute-start(bf16[1024,512]{1,0:T(8,128)(2,1)S(1)} %get-tuple-element.36), channel_id=1, source_target_pairs={{0,1},{1,0},{2,3},{3,2},{4,5},{5,4},{6,7},{7,6},{8,9},{9,8},{10,11... | collective-permute-start | bytes 3145736 | tf_op jit(solution)/shard_map/core_exchange/ppermute | solution.py:336
  5.8 2.4 %pack.1 = (bf16[128,112,128]{2,1,0:T(8,128)(2,1)S(1)}, bf16[1024,512]{1,0:T(8,128)(2,1)S(1)}) custom-call(s32[1]{0:T(128)} %bitcast.me, bf16[512,512]{1,0:T(8,128)(2,1)S(1)} %get-tuple-element.28.h, bf16[512,512]{1,0:T(8,128)(2,1)S(1)} %get-tuple-element.29.a, bf16[512,512]{1,0:T(8,128)(2,1)S(1)} %get-tuple-element.30.g, ...), custom_call_target="tpu_custom_call" | custom-call | tf_op jit(solution)/shard_map/pack/pallas_call | solution.py:338
  8.2 0.0 collective-permute-done.got
  8.2 0.3 join.1
  8.5 57.6 %all_to_all.10 = bf16[128,112,128]{2,1,0:T(8,128)(2,1)S(1)} all-to-all(bf16[128,112,128]{2,1,0:T(8,128)(2,1)S(1)} %bitcast.12), channel_id=1, replica_groups=mesh['dev'=128] {'dev'}, dimensions={0} | all-to-all | bytes 7340032 | tf_op jit(solution)/shard_map/rows_to_owners/all_to_all | solution.py:355
  66.1 1.9 %sum_parts.1 = (bf16[64,2,32,128]{3,2,1,0:T(8,128)(2,1)}, bf16[64,2,80,128]{3,2,1,0:T(8,128)(2,1)}) custom-call(bf16[64,2,112,128]{3,2,1,0:T(8,128)(2,1)S(1)} %bitcast.13), custom_call_target="tpu_custom_call" | custom-call | tf_op jit(solution)/shard_map/sum_parts/pallas_call | solution.py:359
  68.0 4.6 %all-to-all-start.1 = ((bf16[128,32,128]{2,1,0:T(8,128)(2,1)}), bf16[128,32,128]{2,1,0:T(8,128)(2,1)S(1)}, u32[]{:S(2)}, u32[]{:S(2)}) async-start(bf16[128,32,128]{2,1,0:T(8,128)(2,1)} %bitcast.16), calls=%async_computation.1 | async-start | bytes 2097152 | tf_op jit(solution)/shard_map/sums_to_all/all_to_all | solution.py:375
  72.6 12.0 %front.1 = (f32[2048,512]{1,0:T(8,128)}, bf16[512,512]{1,0:T(8,128)(2,1)}) custom-call(bf16[128,80,128]{2,1,0:T(8,128)(2,1)} %bitcast.20, bf16[512,512]{1,0:T(8,128)(2,1)} %get-tuple-element.39.g, bf16[512,512]{1,0:T(8,128)(2,1)} %ws.1), custom_call_target="tpu_custom_call" | custom-call | flops 4831838208 | bytes 8388608 | tf_op jit(solution)/shard_map/front/pallas_call | solution.py:379
  84.6 7.3 %all-to-all-done.1 = bf16[128,32,128]{2,1,0:T(8,128)(2,1)S(1)} async-done(((bf16[128,32,128]{2,1,0:T(8,128)(2,1)}), bf16[128,32,128]{2,1,0:T(8,128)(2,1)S(1)}, u32[]{:S(2)}, u32[]{:S(2)}) %all-to-all-start.1) | async-done | bytes 1048608 | tf_op jit(solution)/shard_map/sums_to_all/all_to_all | solution.py:375
  91.9 0.9 collective-permute-start.1
  92.8 1.4 %fill_own.1 = (f32[1024,512]{1,0:T(8,128)}, f32[512,512]{1,0:T(8,128)}, f32[512,512]{1,0:T(8,128)}) custom-call(s32[1]{0:T(128)} %bitcast.me, bf16[64,2,32,128]{3,2,1,0:T(8,128)(2,1)S(1)} %bitcast.14), custom_call_target="tpu_custom_call" | custom-call | flops 524288 | bytes 3145728 | tf_op jit(solution)/shard_map/fill_own/pallas_call | solution.py:411
  94.2 0.9 collective-permute-done.1
  95.1 1.4 %fill_other.1 = (f32[1024,512]{1,0:T(8,128)}, f32[512,512]{1,0:T(8,128)}, f32[512,512]{1,0:T(8,128)}) custom-call(s32[1]{0:T(128)} %bitcast.me, bf16[64,2,32,128]{3,2,1,0:T(8,128)(2,1)S(1)} %bitcast.15, f32[1024,512]{1,0:T(8,128)} %get-tuple-element.45.refs_0_, ...), custom_call_target="tpu_custom_call", output_to_operand_aliasing={{0}: (2, {}), {1}: (3, {}), {2}: (4, {})} | custom-call | flops 524288 | bytes 3145728 | tf_op jit(solution)/shard_map/fill_other/pallas_call | solution.py:411
Async XLA Ops:
  4.3 3.9 %collective-permute-start = (bf16[1024,512]{1,0:T(8,128)(2,1)S(1)}, bf16[1024,512]{1,0:T(8,128)(2,1)S(1)}, u32[]{:S(2)}, u32[]{:S(2)}) collective-permute-start(bf16[1024,512]{1,0:T(8,128)(2,1)S(1)} %get-tuple-element.36), channel_id=1, source_target_pairs={{0,1},{1,0},{2,3},{3,2},{4,5},{5,4},{6,7},{7,6},{8,9},{9,8},{10,11... | collective-permute-start | bytes 3145736 | tf_op jit(solution)/shard_map/core_exchange/ppermute | solution.py:336
  68.0 23.9 %all-to-all-start.1 = ((bf16[128,32,128]{2,1,0:T(8,128)(2,1)}), bf16[128,32,128]{2,1,0:T(8,128)(2,1)S(1)}, u32[]{:S(2)}, u32[]{:S(2)}) async-start(bf16[128,32,128]{2,1,0:T(8,128)(2,1)} %bitcast.16), calls=%async_computation.1 | async-start | bytes 2097152 | tf_op jit(solution)/shard_map/sums_to_all/all_to_all | solution.py:375
  91.9 3.2 %collective-permute-start.1 = (bf16[128,32,128]{2,1,0:T(8,128)(2,1)S(1)}, bf16[128,32,128]{2,1,0:T(8,128)(2,1)S(1)}, u32[]{:S(2)}, u32[]{:S(2)}) collective-permute-start(bf16[128,32,128]{2,1,0:T(8,128)(2,1)S(1)} %all-to-all-done.1), channel_id=1, source_target_pairs={{0,1},{1,0},{2,3},{3,2},{4,5},{5,4},{6,7},{7,6},{8,9},{9,8},{10,11... | collective-permute-start | bytes 3145736 | tf_op jit(solution)/shard_map/core_exchange_back/ppermute | solution.py:406

commit v8 on v7

--- a/solution.py
+++ b/solution.py
@@ -106,7 +106,7 @@
 
 def grads_kernel(
     me, h_in, a_in, go_in, ws_in, wn_in, hub_in, owner_in, slot_in,
-    g_out, h, a, g, hub, message, send, places, kinds,
+    h, a, g, hub, message, send, places, kinds,
     go, ws, wn, owner, slot, arrived,
 ):
     loads = [
@@ -133,12 +133,9 @@
     loads[6].wait()
     sig = jax.nn.sigmoid(pre)
     g[...] = (go[...].astype(F32) * (sig * (1.0 + pre * (1.0 - sig)))).astype(BF)
-    store = pltpu.make_async_copy(g, g_out, arrived.at[8])
-    store.start()
     message[...] = (mm_nt(g[...], wn[...]) / FANOUT).astype(BF)
     loads[7].wait()
     half_sums(lax.rem(me[0], 2) == 1, message, hub, h, a, g, send)
-    store.wait()
 
 
 def spread_rows():
@@ -153,7 +150,9 @@
     return onehot((at == places[0]) | (at == places[1]) | (at == places[2]))
 
 
-def pack_kernel(me, h, a, g, hub, message, places, kinds, out, mine):
+def pack_kernel(me, h, a, g, hub, message, places, kinds, out, mine, g_out, stored):
+    store = pltpu.make_async_copy(g, g_out, stored)
+    store.start()
     t = message.shape[0]
     n = out.shape[0]
     half_sums(lax.rem(me[0], 2) == 0, message, hub, h, a, g, mine)
@@ -181,6 +180,7 @@
     rows = mm(picks(main, lax.broadcasted_iota(I16, (n * MAIN, t), 0)), msg).astype(BF)
     for q in range(4):
         out[:, q * 16 : (q + 1) * 16, :] = rows[:, q * 128 : (q + 1) * 128].reshape(n, 16, 128)
+    store.wait()
 
 
 def join_kernel(mine, got, held, out):
@@ -307,10 +307,9 @@
     swap = [(i, i ^ 1) for i in range(n)]
 
     with jax.named_scope("grads"):
-        g_kept, h, a, g, hub, message, send, places, kinds = pl.pallas_call(
+        h, a, g, hub, message, send, places, kinds = pl.pallas_call(
             grads_kernel,
             out_shape=(
-                pltpu.HBM((t, width), BF),
                 pltpu.VMEM((t, width), BF),
                 pltpu.VMEM((t, width), BF),
                 pltpu.VMEM((t, width), BF),
@@ -321,25 +320,30 @@
                 pltpu.VMEM((n, 512), BF),
             ),
             in_specs=[SMEM] + [HBM] * 8,
-            out_specs=[HBM] + [VMEM] * 8,
+            out_specs=[VMEM] * 8,
             scratch_shapes=[
                 pltpu.VMEM((t, width), BF),
                 pltpu.VMEM((width, width), BF),
                 pltpu.VMEM((width, width), BF),
                 pltpu.VMEM(owner_t.shape, I32),
                 pltpu.VMEM(slot_t.shape, I32),
-                pltpu.SemaphoreType.DMA((9,)),
+                pltpu.SemaphoreType.DMA((8,)),
             ],
             compiler_params=PARAMS,
         )(me, *map(in_hbm, (h_self, agg, grad_out, w_self, w_neigh, hub_t, owner_t, slot_t)))
     with jax.named_scope("core_exchange"):
         got = lax.ppermute(send, "dev", swap)
     with jax.named_scope("pack"):
-        packed, mine = pl.pallas_call(
+        packed, mine, g_kept = pl.pallas_call(
             pack_kernel,
-            out_shape=(pltpu.VMEM((n, CHUNK, 128), BF), pltpu.VMEM((HUBS, width), BF)),
+            out_shape=(
+                pltpu.VMEM((n, CHUNK, 128), BF),
+                pltpu.VMEM((HUBS, width), BF),
+                pltpu.HBM((t, width), BF),
+            ),
             in_specs=[SMEM] + [VMEM] * 7,
-            out_specs=[VMEM] * 2,
+            out_specs=[VMEM] * 2 + [HBM],
+            scratch_shapes=[pltpu.SemaphoreType.DMA],
             compiler_params=PARAMS,
         )(me, *map(in_vmem, (h, a, g, hub, message, places, kinds)))
     with jax.named_scope("join"):

time: 96.7 us -> 96.7 us (level)
  no operation moved by 1% of the time
where the time goes in v8:
time: 96.7 us; the launch traced here: 96.5 us
  blocking collectives  57.6 us (60%)
  Pallas kernels  23 us (24%)
  waiting for transfers between devices  8.18 us (8%)
  starting transfers between devices  7 us (7%)
    all_to_all x1, blocking collectives, body(): lax.all_to_all(packed.reshape(n, CHUNK, 128), 'dev', split_axis=0, concat...  57.6 us
    pallas_call x1, Pallas kernels, body(): pl.pallas_call(front_kernel, out_shape=(jax.ShapeDtypeStruct((OWN_DEV, wi...  12 us
    all_to_all x1, waiting for transfers between devices, body(): lax.all_to_all(total.reshape(n, 32, 128), 'dev', split_axis=0, concat_axi...  7.3 us
    all_to_all x1, starting transfers between devices, body(): lax.all_to_all(total.reshape(n, 32, 128), 'dev', split_axis=0, concat_axi...  4.6 us
    pallas_call x1, Pallas kernels, body(): pl.pallas_call(grads_kernel, out_shape=(pltpu.VMEM((t, width), BF), pltpu...  3.63 us
    pallas_call x2, Pallas kernels, body(): pl.pallas_call(functools.partial(fill_kernel, scale, mine_too), out_shape...  2.82 us
    pallas_call x1, Pallas kernels, body(): pl.pallas_call(pack_kernel, out_shape=(pltpu.VMEM((n, CHUNK, 128), BF), p...  2.39 us
  transfers between devices with their start and end apart: 3, of which 2 were waited for; matrix products, arithmetic and copies ran while one was open for 0% of the time, Pallas kernels for 16%

profile of v8, /device:TPU:1, one launch (start us, length us, event | category | flops | bytes accessed | tf_op | source)
XLA Modules:
  0.0 96.5 jit_solution(783095696236713619)
XLA Ops:
  0.6 3.6 %grads.1 = (bf16[512,512]{1,0:T(8,128)(2,1)S(1)}, bf16[512,512]{1,0:T(8,128)(2,1)S(1)}, bf16[512,512]{1,0:T(8,128)(2,1)S(1)}, s32[2,512]{1,0:T(2,128)S(1)}, bf16...) custom-call(s32[1]{0:T(128)} %bitcast.me, ...), custom_call_target="tpu_custom_call" | custom-call | tf_op jit(solution)/shard_map/grads/pallas_call | solution.py:310
  4.3 1.5 %collective-permute-start = (bf16[1024,512]{1,0:T(8,128)(2,1)S(1)}, bf16[1024,512]{1,0:T(8,128)(2,1)S(1)}, u32[]{:S(2)}, u32[]{:S(2)}) collective-permute-start(bf16[1024,512]{1,0:T(8,128)(2,1)S(1)} %get-tuple-element.36), channel_id=1, source_target_pairs={{0,1},{1,0},{2,3},{3,2},{4,5},{5,4},{6,7},{7,6},{8,9},{9,8},{10,11... | collective-permute-start | bytes 3145736 | tf_op jit(solution)/shard_map/core_exchange/ppermute | solution.py:335
  5.8 2.4 %pack.1 = (bf16[128,112,128]{2,1,0:T(8,128)(2,1)S(1)}, bf16[1024,512]{1,0:T(8,128)(2,1)S(1)}, bf16[512,512]{1,0:T(8,128)(2,1)}) custom-call(s32[1]{0:T(128)} %bitcast.me, bf16[512,512]{1,0:T(8,128)(2,1)S(1)} %get-tuple-element.28.h, bf16[512,512]{1,0:T(8,128)(2,1)S(1)} %get-tuple-element.29.a, bf16[512,512]{1,0:T(8,128)(2,1)S(1)} %get-tuple-element.30.g, ...), custom_call_target="tpu_custom_call" | custom-call | tf_op jit(solution)/shard_map/pack/pallas_call | solution.py:337
  8.2 0.0 collective-permute-done.got
  8.2 0.3 join.1
  8.5 57.6 %all_to_all.10 = bf16[128,112,128]{2,1,0:T(8,128)(2,1)S(1)} all-to-all(bf16[128,112,128]{2,1,0:T(8,128)(2,1)S(1)} %bitcast.12), channel_id=1, replica_groups=mesh['dev'=128] {'dev'}, dimensions={0} | all-to-all | bytes 7340032 | tf_op jit(solution)/shard_map/rows_to_owners/all_to_all | solution.py:359
  66.1 1.9 %sum_parts.1 = (bf16[64,2,32,128]{3,2,1,0:T(8,128)(2,1)}, bf16[64,2,80,128]{3,2,1,0:T(8,128)(2,1)}) custom-call(bf16[64,2,112,128]{3,2,1,0:T(8,128)(2,1)S(1)} %bitcast.13), custom_call_target="tpu_custom_call" | custom-call | tf_op jit(solution)/shard_map/sum_parts/pallas_call | solution.py:363
  68.0 4.6 %all-to-all-start.1 = ((bf16[128,32,128]{2,1,0:T(8,128)(2,1)}), bf16[128,32,128]{2,1,0:T(8,128)(2,1)S(1)}, u32[]{:S(2)}, u32[]{:S(2)}) async-start(bf16[128,32,128]{2,1,0:T(8,128)(2,1)} %bitcast.16), calls=%async_computation.1 | async-start | bytes 2097152 | tf_op jit(solution)/shard_map/sums_to_all/all_to_all | solution.py:379
  72.6 12.0 %front.1 = (f32[2048,512]{1,0:T(8,128)}, bf16[512,512]{1,0:T(8,128)(2,1)}) custom-call(bf16[128,80,128]{2,1,0:T(8,128)(2,1)} %bitcast.20, bf16[512,512]{1,0:T(8,128)(2,1)} %get-tuple-element.39.g, bf16[512,512]{1,0:T(8,128)(2,1)} %ws.1), custom_call_target="tpu_custom_call" | custom-call | flops 4831838208 | bytes 8388608 | tf_op jit(solution)/shard_map/front/pallas_call | solution.py:383
  84.6 7.3 %all-to-all-done.1 = bf16[128,32,128]{2,1,0:T(8,128)(2,1)S(1)} async-done(((bf16[128,32,128]{2,1,0:T(8,128)(2,1)}), bf16[128,32,128]{2,1,0:T(8,128)(2,1)S(1)}, u32[]{:S(2)}, u32[]{:S(2)}) %all-to-all-start.1) | async-done | bytes 1048608 | tf_op jit(solution)/shard_map/sums_to_all/all_to_all | solution.py:379
  91.9 0.9 collective-permute-start.1
  92.8 1.4 %fill_own.1 = (f32[1024,512]{1,0:T(8,128)}, f32[512,512]{1,0:T(8,128)}, f32[512,512]{1,0:T(8,128)}) custom-call(s32[1]{0:T(128)} %bitcast.me, bf16[64,2,32,128]{3,2,1,0:T(8,128)(2,1)S(1)} %bitcast.14), custom_call_target="tpu_custom_call" | custom-call | flops 524288 | bytes 3145728 | tf_op jit(solution)/shard_map/fill_own/pallas_call | solution.py:415
  94.2 0.9 collective-permute-done.1
  95.1 1.4 %fill_other.1 = (f32[1024,512]{1,0:T(8,128)}, f32[512,512]{1,0:T(8,128)}, f32[512,512]{1,0:T(8,128)}) custom-call(s32[1]{0:T(128)} %bitcast.me, bf16[64,2,32,128]{3,2,1,0:T(8,128)(2,1)S(1)} %bitcast.15, f32[1024,512]{1,0:T(8,128)} %get-tuple-element.45.refs_0_, ...), custom_call_target="tpu_custom_call", output_to_operand_aliasing={{0}: (2, {}), {1}: (3, {}), {2}: (4, {})} | custom-call | flops 524288 | bytes 3145728 | tf_op jit(solution)/shard_map/fill_other/pallas_call | solution.py:415
Async XLA Ops:
  4.3 3.9 %collective-permute-start = (bf16[1024,512]{1,0:T(8,128)(2,1)S(1)}, bf16[1024,512]{1,0:T(8,128)(2,1)S(1)}, u32[]{:S(2)}, u32[]{:S(2)}) collective-permute-start(bf16[1024,512]{1,0:T(8,128)(2,1)S(1)} %get-tuple-element.36), channel_id=1, source_target_pairs={{0,1},{1,0},{2,3},{3,2},{4,5},{5,4},{6,7},{7,6},{8,9},{9,8},{10,11... | collective-permute-start | bytes 3145736 | tf_op jit(solution)/shard_map/core_exchange/ppermute | solution.py:335
  68.0 23.9 %all-to-all-start.1 = ((bf16[128,32,128]{2,1,0:T(8,128)(2,1)}), bf16[128,32,128]{2,1,0:T(8,128)(2,1)S(1)}, u32[]{:S(2)}, u32[]{:S(2)}) async-start(bf16[128,32,128]{2,1,0:T(8,128)(2,1)} %bitcast.16), calls=%async_computation.1 | async-start | bytes 2097152 | tf_op jit(solution)/shard_map/sums_to_all/all_to_all | solution.py:379
  91.9 3.2 %collective-permute-start.1 = (bf16[128,32,128]{2,1,0:T(8,128)(2,1)S(1)}, bf16[128,32,128]{2,1,0:T(8,128)(2,1)S(1)}, u32[]{:S(2)}, u32[]{:S(2)}) collective-permute-start(bf16[128,32,128]{2,1,0:T(8,128)(2,1)S(1)} %all-to-all-done.1), channel_id=1, source_target_pairs={{0,1},{1,0},{2,3},{3,2},{4,5},{5,4},{6,7},{7,6},{8,9},{9,8},{10,11... | collective-permute-start | bytes 3145736 | tf_op jit(solution)/shard_map/core_exchange_back/ppermute | solution.py:410

commit v9 on v8

--- a/solution.py
+++ b/solution.py
@@ -133,7 +133,7 @@
     loads[6].wait()
     sig = jax.nn.sigmoid(pre)
     g[...] = (go[...].astype(F32) * (sig * (1.0 + pre * (1.0 - sig)))).astype(BF)
-    message[...] = (mm_nt(g[...], wn[...]) / FANOUT).astype(BF)
+    message[...] = (mm_nt(g[...], wn[...]) * (1.0 / FANOUT)).astype(BF)
     loads[7].wait()
     half_sums(lax.rem(me[0], 2) == 1, message, hub, h, a, g, send)
 

time: 96.7 us -> 96.7 us (level)
  no operation moved by 1% of the time
where the time goes in v9:
time: 96.7 us; the launch traced here: 96.5 us
  blocking collectives  57.6 us (60%)
  Pallas kernels  23 us (24%)
  waiting for transfers between devices  8.18 us (8%)
  starting transfers between devices  7 us (7%)
    all_to_all x1, blocking collectives, body(): lax.all_to_all(packed.reshape(n, CHUNK, 128), 'dev', split_axis=0, concat...  57.6 us
    pallas_call x1, Pallas kernels, body(): pl.pallas_call(front_kernel, out_shape=(jax.ShapeDtypeStruct((OWN_DEV, wi...  12 us
    all_to_all x1, waiting for transfers between devices, body(): lax.all_to_all(total.reshape(n, 32, 128), 'dev', split_axis=0, concat_axi...  7.3 us
    all_to_all x1, starting transfers between devices, body(): lax.all_to_all(total.reshape(n, 32, 128), 'dev', split_axis=0, concat_axi...  4.6 us
    pallas_call x1, Pallas kernels, body(): pl.pallas_call(grads_kernel, out_shape=(pltpu.VMEM((t, width), BF), pltpu...  3.63 us
    pallas_call x2, Pallas kernels, body(): pl.pallas_call(functools.partial(fill_kernel, scale, mine_too), out_shape...  2.82 us
    pallas_call x1, Pallas kernels, body(): pl.pallas_call(pack_kernel, out_shape=(pltpu.VMEM((n, CHUNK, 128), BF), p...  2.39 us
  transfers between devices with their start and end apart: 3, of which 2 were waited for; matrix products, arithmetic and copies ran while one was open for 0% of the time, Pallas kernels for 16%

profile of v9, /device:TPU:1, one launch (start us, length us, event | category | flops | bytes accessed | tf_op | source)
XLA Modules:
  0.0 96.5 jit_solution(783095696236713619)
XLA Ops:
  0.6 3.6 %grads.1 = (bf16[512,512]{1,0:T(8,128)(2,1)S(1)}, bf16[512,512]{1,0:T(8,128)(2,1)S(1)}, bf16[512,512]{1,0:T(8,128)(2,1)S(1)}, s32[2,512]{1,0:T(2,128)S(1)}, bf16...) custom-call(s32[1]{0:T(128)} %bitcast.me, ...), custom_call_target="tpu_custom_call" | custom-call | tf_op jit(solution)/shard_map/grads/pallas_call | solution.py:310
  4.3 1.5 %collective-permute-start = (bf16[1024,512]{1,0:T(8,128)(2,1)S(1)}, bf16[1024,512]{1,0:T(8,128)(2,1)S(1)}, u32[]{:S(2)}, u32[]{:S(2)}) collective-permute-start(bf16[1024,512]{1,0:T(8,128)(2,1)S(1)} %get-tuple-element.36), channel_id=1, source_target_pairs={{0,1},{1,0},{2,3},{3,2},{4,5},{5,4},{6,7},{7,6},{8,9},{9,8},{10,11... | collective-permute-start | bytes 3145736 | tf_op jit(solution)/shard_map/core_exchange/ppermute | solution.py:335
  5.8 2.4 %pack.1 = (bf16[128,112,128]{2,1,0:T(8,128)(2,1)S(1)}, bf16[1024,512]{1,0:T(8,128)(2,1)S(1)}, bf16[512,512]{1,0:T(8,128)(2,1)}) custom-call(s32[1]{0:T(128)} %bitcast.me, bf16[512,512]{1,0:T(8,128)(2,1)S(1)} %get-tuple-element.28.h, bf16[512,512]{1,0:T(8,128)(2,1)S(1)} %get-tuple-element.29.a, bf16[512,512]{1,0:T(8,128)(2,1)S(1)} %get-tuple-element.30.g, ...), custom_call_target="tpu_custom_call" | custom-call | tf_op jit(solution)/shard_map/pack/pallas_call | solution.py:337
  8.2 0.0 collective-permute-done.got
  8.2 0.3 join.1
  8.5 57.6 %all_to_all.10 = bf16[128,112,128]{2,1,0:T(8,128)(2,1)S(1)} all-to-all(bf16[128,112,128]{2,1,0:T(8,128)(2,1)S(1)} %bitcast.12), channel_id=1, replica_groups=mesh['dev'=128] {'dev'}, dimensions={0} | all-to-all | bytes 7340032 | tf_op jit(solution)/shard_map/rows_to_owners/all_to_all | solution.py:359
  66.1 1.9 %sum_parts.1 = (bf16[64,2,32,128]{3,2,1,0:T(8,128)(2,1)}, bf16[64,2,80,128]{3,2,1,0:T(8,128)(2,1)}) custom-call(bf16[64,2,112,128]{3,2,1,0:T(8,128)(2,1)S(1)} %bitcast.13), custom_call_target="tpu_custom_call" | custom-call | tf_op jit(solution)/shard_map/sum_parts/pallas_call | solution.py:363
  68.0 4.6 %all-to-all-start.1 = ((bf16[128,32,128]{2,1,0:T(8,128)(2,1)}), bf16[128,32,128]{2,1,0:T(8,128)(2,1)S(1)}, u32[]{:S(2)}, u32[]{:S(2)}) async-start(bf16[128,32,128]{2,1,0:T(8,128)(2,1)} %bitcast.16), calls=%async_computation.1 | async-start | bytes 2097152 | tf_op jit(solution)/shard_map/sums_to_all/all_to_all | solution.py:379
  72.6 12.0 %front.1 = (f32[2048,512]{1,0:T(8,128)}, bf16[512,512]{1,0:T(8,128)(2,1)}) custom-call(bf16[128,80,128]{2,1,0:T(8,128)(2,1)} %bitcast.20, bf16[512,512]{1,0:T(8,128)(2,1)} %get-tuple-element.39.g, bf16[512,512]{1,0:T(8,128)(2,1)} %ws.1), custom_call_target="tpu_custom_call" | custom-call | flops 4831838208 | bytes 8388608 | tf_op jit(solution)/shard_map/front/pallas_call | solution.py:383
  84.6 7.3 %all-to-all-done.1 = bf16[128,32,128]{2,1,0:T(8,128)(2,1)S(1)} async-done(((bf16[128,32,128]{2,1,0:T(8,128)(2,1)}), bf16[128,32,128]{2,1,0:T(8,128)(2,1)S(1)}, u32[]{:S(2)}, u32[]{:S(2)}) %all-to-all-start.1) | async-done | bytes 1048608 | tf_op jit(solution)/shard_map/sums_to_all/all_to_all | solution.py:379
  91.9 0.9 collective-permute-start.1
  92.8 1.4 %fill_own.1 = (f32[1024,512]{1,0:T(8,128)}, f32[512,512]{1,0:T(8,128)}, f32[512,512]{1,0:T(8,128)}) custom-call(s32[1]{0:T(128)} %bitcast.me, bf16[64,2,32,128]{3,2,1,0:T(8,128)(2,1)S(1)} %bitcast.14), custom_call_target="tpu_custom_call" | custom-call | flops 524288 | bytes 3145728 | tf_op jit(solution)/shard_map/fill_own/pallas_call | solution.py:415
  94.2 0.9 collective-permute-done.1
  95.1 1.4 %fill_other.1 = (f32[1024,512]{1,0:T(8,128)}, f32[512,512]{1,0:T(8,128)}, f32[512,512]{1,0:T(8,128)}) custom-call(s32[1]{0:T(128)} %bitcast.me, bf16[64,2,32,128]{3,2,1,0:T(8,128)(2,1)S(1)} %bitcast.15, f32[1024,512]{1,0:T(8,128)} %get-tuple-element.45.refs_0_, ...), custom_call_target="tpu_custom_call", output_to_operand_aliasing={{0}: (2, {}), {1}: (3, {}), {2}: (4, {})} | custom-call | flops 524288 | bytes 3145728 | tf_op jit(solution)/shard_map/fill_other/pallas_call | solution.py:415
Async XLA Ops:
  4.3 3.9 %collective-permute-start = (bf16[1024,512]{1,0:T(8,128)(2,1)S(1)}, bf16[1024,512]{1,0:T(8,128)(2,1)S(1)}, u32[]{:S(2)}, u32[]{:S(2)}) collective-permute-start(bf16[1024,512]{1,0:T(8,128)(2,1)S(1)} %get-tuple-element.36), channel_id=1, source_target_pairs={{0,1},{1,0},{2,3},{3,2},{4,5},{5,4},{6,7},{7,6},{8,9},{9,8},{10,11... | collective-permute-start | bytes 3145736 | tf_op jit(solution)/shard_map/core_exchange/ppermute | solution.py:335
  68.0 23.9 %all-to-all-start.1 = ((bf16[128,32,128]{2,1,0:T(8,128)(2,1)}), bf16[128,32,128]{2,1,0:T(8,128)(2,1)S(1)}, u32[]{:S(2)}, u32[]{:S(2)}) async-start(bf16[128,32,128]{2,1,0:T(8,128)(2,1)} %bitcast.16), calls=%async_computation.1 | async-start | bytes 2097152 | tf_op jit(solution)/shard_map/sums_to_all/all_to_all | solution.py:379
  91.9 3.2 %collective-permute-start.1 = (bf16[128,32,128]{2,1,0:T(8,128)(2,1)S(1)}, bf16[128,32,128]{2,1,0:T(8,128)(2,1)S(1)}, u32[]{:S(2)}, u32[]{:S(2)}) collective-permute-start(bf16[128,32,128]{2,1,0:T(8,128)(2,1)S(1)} %all-to-all-done.1), channel_id=1, source_target_pairs={{0,1},{1,0},{2,3},{3,2},{4,5},{5,4},{6,7},{7,6},{8,9},{9,8},{10,11... | collective-permute-start | bytes 3145736 | tf_op jit(solution)/shard_map/core_exchange_back/ppermute | solution.py:410
